TPU v7x, 256 devices: a whole 4x4x8 slice. The times are simulated.
256 devices in a mesh: blk: 64 (over z, y_lo, x), win: 4 (over y_hi, core).
Axes of the slice: x: 4, y: 4 (y_hi: 2, y_lo: 2; y = y_hi * 2 + y_lo), z: 8, core: 2. Of those that a mesh axis runs over, the one named last changes fastest.
Arguments:
- raw_traces: bfloat16 [64, 1024, 8192], P('win', None, 'blk'), may hold values from -45 to 45, as said below
- channel_mask: int32 [64, 8192], P('win', 'blk'), may hold values 0 or 1
Outputs:
- cross_first: bfloat16 [256, 2, 8192, 128], P('win', None, 'blk')
- cross_second: bfloat16 [256, 2, 8192, 128], P('win', None, 'blk')
Inputs may be any that keep to these rules, and one draw needn't show every extreme that they name: `raw_traces`: each channel has its own gain and each window its own level; all channels share part of the wavefield.
All inputs are finite; a program needn't handle non-finite values. No bound on the sum of `channel_mask` on one device may be relied on, other than what follows from the above.
Results may differ from a plain program's by a relative error of at most 0.0051.
Values may be sent and summed in bfloat16 or wider, within the bound.
No kernel may reach another device: no remote copies, remote signals or barrier semaphores. Data moves between devices by JAX's collectives and lax.ppermute only.
A program may use at most 128 MiB of HBM per device.

v0:
```python
import math

import jax
import jax.numpy as jnp
from jax import lax
from jax.sharding import PartitionSpec as P

BINS = 256
SAMPLES = 1024
LOW = 32
BAND = 64


def swapped(block, axis, stride):
    count = lax.axis_size(axis)
    route = []
    for low in range(count):
        high = low | 1 << stride
        if high != low and high < count:
            route += [(low, high), (high, low)]
    return lax.ppermute(block, axis, route)


def make_twiddles():
    sample_index = jnp.arange(SAMPLES, dtype=jnp.int32)
    bin_index = LOW + jnp.arange(BINS, dtype=jnp.int32)
    phase_step = sample_index[:, None] * bin_index[None, :] % SAMPLES
    angles = phase_step.astype(jnp.float32) * (2.0 * math.pi / SAMPLES)
    return jnp.stack([jnp.cos(angles), -jnp.sin(angles)], axis=1).astype(jnp.bfloat16)


def whiten_block(traces, mask_rows):
    spectra = jnp.einsum(
        "wtc,tkf->wkfc", traces, make_twiddles(), preferred_element_type=jnp.float32
    )
    power_sum = spectra[:, 0] * spectra[:, 0] + spectra[:, 1] * spectra[:, 1]
    window_count = power_sum.shape[0]
    band_power = jnp.mean(
        power_sum.reshape(window_count, BINS // BAND, BAND, power_sum.shape[2]), axis=2
    )
    band_scale = jnp.repeat(lax.rsqrt(band_power + 1e-06), BAND, axis=1)
    weights = band_scale * mask_rows.astype(jnp.float32)[:, None, :]
    return (spectra * weights[:, None]).astype(jnp.bfloat16)


def cross_block(own_bins, other_bins):
    products = jnp.einsum(
        "wkfi,wlfj->fkilj", own_bins, other_bins, preferred_element_type=jnp.float32
    )
    real_part = products[:, 0, :, 0, :] + products[:, 1, :, 1, :]
    imag_part = products[:, 1, :, 0, :] - products[:, 0, :, 1, :]
    stacked = jnp.stack([real_part, imag_part], axis=1) * (1.0 / math.sqrt(own_bins.shape[0]))
    return stacked.astype(jnp.bfloat16)


def body(raw_traces, channel_mask):
    whitened = whiten_block(raw_traces, channel_mask)
    bit_count = lax.axis_size("blk").bit_length() - 1
    round_bits = (bit_count - 1, 0)
    own_bins = lax.all_to_all(whitened, "win", split_axis=2, concat_axis=0, tiled=True)
    results = []
    for round_bit in round_bits:
        partner_bins = swapped(own_bins, "blk", round_bit)
        results.append(cross_block(own_bins, partner_bins))
    return (results[0], results[1])


def solution(mesh):
    in_specs = (P("win", None, "blk"), P("win", "blk"))
    out_specs = (P("win", None, "blk", None), P("win", None, "blk", None))
    return jax.shard_map(body, mesh=mesh, in_specs=in_specs, out_specs=out_specs, check_vma=False)
```

profile of v0, /device:TPU:38, one launch (start us, length us, event | category | flops | bytes accessed | tf_op | source)
XLA Modules:
  0.0 185.3 jit_solution(2366319046921261611)
XLA Ops:
  0.6 4.9 %cosine_convert_fusion = (bf16[1024,1,256]{0,2,1:T(8,128)(2,1)S(1)}, bf16[1024,1,256]{0,2,1:T(8,128)(2,1)S(1)}) fusion(s32[256]{0:T(256)S(1)} %iota_add_fusion), kind=kLoop, calls=%fused_computation.37 | loop fusion | flops 4456448 | bytes 1049600 | tf_op jit(solution)/shard_map/convert
  5.5 6.6 %fusion.9 = f32[16,2,256,128]{3,2,0,1:T(8,128)} fusion(bf16[16,1024,128]{2,1,0:T(8,128)(2,1)} %param.2, bf16[1024,1,256]{0,2,1:T(8,128)(2,1)S(1)} %get-tuple-element.9, bf16[1024,1,256]{0,2,1:T(8,128)(2,1)S(1)} %get-tuple-element.8), kind=kOutput, calls=%fused_computation.17 | convolution fusion | flops 2149580800 | bytes 9437184 | tf_op jit(solution)/shard_map/wtc,tkf->wkfc/dot_general | solution.py:33
  12.1 0.0 copy-start.1
  12.1 2.5 %fusion.12 = f32[16,1,256,128]{3,2,0,1:T(8,128)S(1)} fusion(f32[16,2,256,128]{3,2,0,1:T(8,128)} %fusion.9), kind=kLoop, calls=%fused_computation.19 | loop fusion | flops 1572864 | bytes 6291456 | tf_op jit(solution)/shard_map/add | solution.py:36
  14.5 0.3 reduce_sum.9
  14.8 0.0 copy-done.1
  14.9 0.1 bitcast_multiply_fusion
  15.0 2.6 %multiply_convert_fusion = bf16[16,2,256,128]{3,2,0,1:T(8,128)(2,1)S(1)} fusion(f32[16,2,256,128]{3,2,0,1:T(8,128)} %fusion.9, f32[16,256,128]{2,1,0:T(8,128)S(1)} %bitcast_multiply_fusion), kind=kLoop, calls=%fused_computation.16 | loop fusion | flops 2097152 | bytes 8388608 | tf_op jit(solution)/shard_map/convert_element_type | solution.py:43
  17.6 1.4 copy.13
  19.0 31.5 %all_to_all.18 = bf16[16,2,256,128]{3,0,1,2:T(8,128)(2,1)S(1)} all-to-all(bf16[16,2,256,128]{3,0,1,2:T(8,128)(2,1)S(1)} %copy.13), channel_id=1, replica_groups=mesh['blk'=64,'win'=4] {'win'}, dimensions={2} | all-to-all | bytes 4194304 | tf_op jit(solution)/shard_map/all_to_all | solution.py:60
  50.5 0.6 copy.14
  51.1 6.4 %collective-permute-start = (bf16[64,2,64,128]{3,0,1,2:T(8,128)(2,1)S(1)}, bf16[64,2,64,128]{3,0,1,2:T(8,128)(2,1)S(1)}, u32[]{:S(2)}, u32[]{:S(2)}) collective-permute-start(bf16[64,2,64,128]{3,0,1,2:T(8,128)(2,1)S(1)} %bitcast.51), channel_id=1, source_target_pairs={{0,128},{128,0},{4,132},{132,4},{8,136},{136,8},{12,140},{140,12},... | collective-permute-start | bytes 6291464 | tf_op jit(solution)/shard_map/ppermute | solution.py:21
  57.5 0.8 collective-permute-start.1
  58.3 89.8 %collective-permute-done = bf16[64,2,64,128]{3,0,1,2:T(8,128)(2,1)S(1)} collective-permute-done((bf16[64,2,64,128]{3,0,1,2:T(8,128)(2,1)S(1)}, bf16[64,2,64,128]{3,0,1,2:T(8,128)(2,1)S(1)}, u32[]{:S(2)}, u32[]{:S(2)}) %collective-permute-start) | collective-permute-done | bytes 2097184 | tf_op jit(solution)/shard_map/ppermute | solution.py:21
  148.1 2.4 %fusion.13 = f32[64,2,128,2,128]{4,2,3,1,0:T(8,128)S(1)} fusion(bf16[64,2,64,128,1]{3,0,4,1,2:T(8,128)(2,1)S(1)} %bitcast.53, bf16[64,2,64,128]{3,0,1,2:T(8,128)(2,1)S(1)} %collective-permute-done), kind=kOutput, calls=%fused_computation.21 | convolution fusion | flops 536870912 | bytes 20971520 | tf_op jit(solution)/shard_map/wkfi,wlfj->fkilj/dot_general | solution.py:47
  150.5 0.9 fusion.4
  151.4 2.8 %fusion.6 = f32[64,1,128,128]{3,2,0,1:T(8,128)} fusion(f32[64,2,128,2,128]{4,2,3,1,0:T(8,128)S(1)} %fusion.13), kind=kLoop, calls=%fused_computation.12 | loop fusion | flops 1048576 | bytes 12582912 | tf_op jit(solution)/shard_map/add | solution.py:50
  154.2 0.0 collective-permute-done.1
  154.2 8.1 %fusion.15 = f32[64,2,128,2,128]{4,2,0,3,1:T(8,128)} fusion(bf16[64,2,64,128,1]{3,0,1,2,4:T(8,128)(2,1)S(1)} %bitcast.54, bf16[64,2,64,128]{3,0,1,2:T(8,128)(2,1)S(1)} %collective-permute-done.1), kind=kOutput, calls=%fused_computation.24 | convolution fusion | flops 536870912 | bytes 20971520 | tf_op jit(solution)/shard_map/wkfi,wlfj->fkilj/dot_general | solution.py:47
  162.3 11.9 %fusion.3 = (f32[64,1,128,128]{3,2,0,1:T(8,128)}, f32[64,1,128,128]{3,2,0,1:T(8,128)}) fusion(f32[64,2,128,2,128]{4,2,0,3,1:T(8,128)} %fusion.15), kind=kLoop, calls=%fused_computation.7 | loop fusion | flops 2097152 | bytes 25165824 | tf_op jit(solution)/shard_map/add | solution.py:50
  174.2 4.0 %fusion.1 = bf16[64,2,128,128]{3,2,0,1:T(8,128)(2,1)S(1)} fusion(f32[64,1,128,128]{3,2,0,1:T(8,128)} %get-tuple-element.7, f32[64,1,128,128]{3,2,0,1:T(8,128)} %get-tuple-element.6), kind=kLoop, calls=%fused_computation.3 | loop fusion | flops 6291456 | bytes 12582912 | tf_op jit(solution)/shard_map/convert_element_type | solution.py:53
  178.2 0.0 copy-start
  178.2 2.4 %copy.22 = bf16[64,2,128,128]{3,2,1,0:T(8,128)(2,1)} copy(bf16[64,2,128,128]{3,2,0,1:T(8,128)(2,1)S(1)} %fusion.1) | data formatting | bytes 8388608
  180.7 1.2 copy-done
  181.9 1.1 fusion
  183.0 2.3 %copy.21 = bf16[64,2,128,128]{3,2,1,0:T(8,128)(2,1)} copy(bf16[64,2,128,128]{3,2,0,1:T(8,128)(2,1)S(1)} %fusion) | data formatting | bytes 8388608
  (3 shorter events, 0.0 us)
Async XLA Ops:
  12.1 2.8 %copy-start.1 = (s32[16,128]{1,0:T(8,128)S(1)}, s32[16,128]{1,0:T(8,128)}, u32[]{:S(2)}) copy-start(s32[16,128]{1,0:T(8,128)} %param.3) | copy-start | bytes 24580
  51.1 97.1 %collective-permute-start = (bf16[64,2,64,128]{3,0,1,2:T(8,128)(2,1)S(1)}, bf16[64,2,64,128]{3,0,1,2:T(8,128)(2,1)S(1)}, u32[]{:S(2)}, u32[]{:S(2)}) collective-permute-start(bf16[64,2,64,128]{3,0,1,2:T(8,128)(2,1)S(1)} %bitcast.51), channel_id=1, source_target_pairs={{0,128},{128,0},{4,132},{132,4},{8,136},{136,8},{12,140},{140,12},... | collective-permute-start | bytes 6291464 | tf_op jit(solution)/shard_map/ppermute | solution.py:21
  57.5 96.7 %collective-permute-start.1 = (bf16[64,2,64,128]{3,0,1,2:T(8,128)(2,1)S(1)}, bf16[64,2,64,128]{3,0,1,2:T(8,128)(2,1)S(1)}, u32[]{:S(2)}, u32[]{:S(2)}) collective-permute-start(bf16[64,2,64,128]{3,0,1,2:T(8,128)(2,1)S(1)} %bitcast.52), channel_id=1, source_target_pairs={{0,4},{4,0},{8,12},{12,8},{16,20},{20,16},{24,28},{28,24},{32,36},... | collective-permute-start | bytes 6291464 | tf_op jit(solution)/shard_map/ppermute | solution.py:21
  178.2 3.7 %copy-start = (f32[64,1,128,128]{3,2,0,1:T(8,128)S(1)}, f32[64,1,128,128]{3,2,0,1:T(8,128)}, u32[]{:S(2)}) copy-start(f32[64,1,128,128]{3,2,0,1:T(8,128)} %fusion.6) | copy-start | bytes 12582916
where the time goes:
time: 186 us; the launch traced here: 185 us
  waiting for transfers between devices  89.8 us (48%)
  blocking collectives  31.5 us (17%)
  other arithmetic  31 us (17%)
  matrix products  17 us (9%)
  local copies, waits for them, and re-layouts  7.99 us (4%)
  starting transfers between devices  7.21 us (4%)
    ppermute x2, waiting for transfers between devices, swapped(): return lax.ppermute(block, axis, route)  89.8 us
    all_to_all x1, blocking collectives, body(): lax.all_to_all(whitened, 'win', split_axis=2, concat_axis=0, tiled=True)  31.5 us
    add x2, other arithmetic, cross_block(): real_part = products[:, 0, :, 0, :] + products[:, 1, :, 1, :]  14.6 us
    dot_general x2, matrix products, cross_block(): jnp.einsum('wkfi,wlfj->fkilj', own_bins, other_bins, preferred_element_ty...  10.5 us
    ppermute x2, starting transfers between devices, swapped(): return lax.ppermute(block, axis, route)  7.21 us
    dot_general x1, matrix products, whiten_block(): jnp.einsum('wtc,tkf->wkfc', traces, make_twiddles(), preferred_element_ty...  6.55 us
    unnamed x6, local copies, waits for them, and re-layouts  6.02 us
    convert_element_type x2, other arithmetic, cross_block(): return stacked.astype(jnp.bfloat16)  5.09 us
  transfers between devices with their start and end apart: 2, of which 1 were waited for; matrix products, arithmetic and copies ran while one was open for 3% of the time, Pallas kernels for 0%

commit v1 on v0

v1 whole, which is shorter than its diff:
```python
import functools
import math

import jax
import jax.numpy as jnp
import ml_dtypes
import numpy as np
from jax import lax
from jax.experimental import pallas as pl
from jax.experimental.pallas import tpu as pltpu
from jax.sharding import PartitionSpec as P

BINS = 256
SAMPLES = 1024
LOW = 32
BAND = 64
BANDS = BINS // BAND
CH = 128
WINS = 16
PAIR = 2
VMEM_LIMIT = 40 * 1024 * 1024


def band_twiddles():
    sample_index = np.arange(SAMPLES, dtype=np.int32)
    bin_index = LOW + np.arange(BINS, dtype=np.int32)
    phase_step = bin_index[:, None] * sample_index[None, :] % SAMPLES
    angles = phase_step.astype(np.float32) * np.float32(2.0 * math.pi / SAMPLES)
    table = np.stack(
        [np.cos(angles).reshape(BANDS, BAND, SAMPLES), -np.sin(angles).reshape(BANDS, BAND, SAMPLES)],
        axis=1,
    )
    return table.reshape(BANDS, 2 * BAND, SAMPLES).astype(ml_dtypes.bfloat16)


def spectra_kernel(parts, band_ref, *refs):
    twiddle_refs = refs[:parts]
    raw_ref, mask_ref = refs[parts], refs[parts + 1]
    out_refs = refs[parts + 2 : 2 * parts + 2]
    wide_refs = refs[2 * parts + 2 :]
    step = pl.program_id(0)
    pair = jnp.concatenate([raw_ref[0], raw_ref[1]], axis=1)
    for part in range(parts):
        spectra = jnp.dot(twiddle_refs[part][0], pair, preferred_element_type=jnp.float32)
        real, imag = spectra[:BAND], spectra[BAND:]
        power = jnp.sum(real * real + imag * imag, axis=0, keepdims=True) * (1.0 / BAND)
        scale = lax.rsqrt(power + 1e-06)
        for half in range(PAIR):
            window = step * PAIR + half
            cols = slice(half * CH, (half + 1) * CH)
            weight = scale[:, cols] * mask_ref[pl.ds(window, 1), :].astype(jnp.float32)
            wide_refs[part][pl.ds(window, BAND, stride=2 * WINS), :] = real[:, cols] * weight
            wide_refs[part][pl.ds(window + WINS, BAND, stride=2 * WINS), :] = imag[:, cols] * weight

    @pl.when(step == pl.num_programs(0) - 1)
    def _():
        for part in range(parts):
            out_refs[part][...] = wide_refs[part][...].astype(jnp.bfloat16)


def whiten_bands(bands, table, raw_traces, channel_mask):
    parts = bands.shape[0]

    def band_spec(part):
        return pl.BlockSpec((1, 2 * BAND, SAMPLES), lambda step, band_ref: (band_ref[part], 0, 0))

    rows = BAND * 2 * WINS
    return pl.pallas_call(
        functools.partial(spectra_kernel, parts),
        out_shape=[jax.ShapeDtypeStruct((rows, CH), jnp.bfloat16)] * parts,
        grid_spec=pltpu.PrefetchScalarGridSpec(
            num_scalar_prefetch=1,
            grid=(WINS // PAIR,),
            in_specs=[band_spec(part) for part in range(parts)]
            + [
                pl.BlockSpec((PAIR, SAMPLES, CH), lambda step, band_ref: (step, 0, 0)),
                pl.BlockSpec((WINS, CH), lambda step, band_ref: (0, 0)),
            ],
            out_specs=[pl.BlockSpec((rows, CH), lambda step, band_ref: (0, 0))] * parts,
            scratch_shapes=[pltpu.VMEM((rows, CH), jnp.float32)] * parts,
        ),
        compiler_params=pltpu.CompilerParams(vmem_limit_bytes=VMEM_LIMIT),
        cost_estimate=pl.CostEstimate(
            flops=2 * WINS * CH * SAMPLES * 2 * BAND * parts,
            bytes_accessed=2 * WINS * CH * SAMPLES + parts * 2 * rows * CH,
            transcendentals=0,
        ),
    )(bands, *([table] * parts), raw_traces, channel_mask)


def cross_kernel(count, bins, *refs):
    own_refs, other_refs, out_ref = refs[:BANDS], refs[BANDS : 2 * BANDS], refs[2 * BANDS]
    scale = 1.0 / math.sqrt(WINS * BANDS)
    for index in range(bins):
        rows = slice(index * 2 * WINS, (index + 1) * 2 * WINS)
        own = [ref[rows, :] for ref in own_refs]
        turned = []
        for piece in own:
            turned += [piece[WINS:], -piece[:WINS]]
        left = jnp.concatenate([jnp.concatenate(own, axis=0), jnp.concatenate(turned, axis=0)], axis=1)
        right = jnp.concatenate([ref[rows, :] for ref in other_refs], axis=0)
        tile = lax.dot_general(left, right, (((0,), (0,)), ((), ())), preferred_element_type=jnp.float32)
        tile = (tile * scale).astype(jnp.bfloat16)
        out_ref[index, 0] = tile[:CH]
        out_ref[index, 1] = tile[CH:]


def cross_blocks(own, other):
    bins = 8
    rows = bins * 2 * WINS
    piece = pl.BlockSpec((rows, CH), lambda step: (step, 0))
    return pl.pallas_call(
        functools.partial(cross_kernel, WINS * BANDS, bins),
        out_shape=jax.ShapeDtypeStruct((BAND, 2, CH, CH), jnp.bfloat16),
        grid=(BAND // bins,),
        in_specs=[piece] * (2 * BANDS),
        out_specs=pl.BlockSpec((bins, 2, CH, CH), lambda step: (step, 0, 0, 0)),
        compiler_params=pltpu.CompilerParams(vmem_limit_bytes=VMEM_LIMIT),
        cost_estimate=pl.CostEstimate(
            flops=2 * BAND * 2 * CH * CH * 2 * WINS * BANDS,
            bytes_accessed=2 * BAND * 2 * CH * CH + 4 * BANDS * BAND * 2 * WINS * CH,
            transcendentals=0,
        ),
    )(*own, *other)


def swap_win(piece, offset):
    return lax.ppermute(piece, "win", [(i, i ^ offset) for i in range(lax.axis_size("win"))])


def swap_blk(piece, stride):
    return lax.ppermute(piece, "blk", [(i, i ^ stride) for i in range(lax.axis_size("blk"))])


def body(raw_traces, channel_mask):
    table = jnp.asarray(band_twiddles())
    mine = lax.axis_index("win").astype(jnp.int32)
    (own_piece,) = whiten_bands(mine[None], table, raw_traces, channel_mask)
    others = jnp.stack([mine ^ offset for offset in range(1, BANDS)])
    leaving = whiten_bands(others, table, raw_traces, channel_mask)
    own = [own_piece] + [swap_win(leaving[offset - 1], offset) for offset in range(1, BANDS)]
    far = lax.axis_size("blk") // 2
    results = []
    for stride in (far, 1):
        other = [swap_blk(piece, stride) for piece in own]
        results.append(cross_blocks(own, other))
    return tuple(results)


def solution(mesh):
    in_specs = (P("win", None, "blk"), P("win", "blk"))
    out_specs = (P("win", None, "blk", None), P("win", None, "blk", None))
    return jax.shard_map(body, mesh=mesh, in_specs=in_specs, out_specs=out_specs, check_vma=False)
```

time: 186 us -> 126 us (0.68)
  blocking collectives: 31.5 us -> 0 us
  other arithmetic: 31 us -> 0.08 us
  Pallas kernels: 0 us -> 19.2 us
  starting transfers between devices: 7.21 us -> 25.9 us
  matrix products: 17 us -> 0 us
  waiting for transfers between devices: 89.8 us -> 75.5 us
  local copies, waits for them, and re-layouts: 7.99 us -> 4.12 us
    all_to_all x1 -> x0, blocking collectives: 31.5 us -> none  [body(): lax.all_to_all(whitened, 'win', split_axis=2, concat_axis=0, tiled=True)]
    pallas_call x0 -> x4, Pallas kernels: none -> 19.2 us  [the longest x2 9.76 us: cross_blocks(): pl.pallas_call(functools.partial(cross_kernel, WINS * BANDS, bins), out_s...]
    ppermute x2 -> x11, starting transfers between devices: 7.21 us -> 25.9 us  [the longest x8 22.4 us: swap_blk(): lax.ppermute(piece, 'blk', [(i, i ^ stride) for i in range(lax.axis_size(...]
    add x4 -> x0, other arithmetic: 17.1 us -> none  [the longest x2 14.6 us: cross_block(): real_part = products[:, 0, :, 0, :] + products[:, 1, :, 1, :]]
    dot_general x3 -> x0, matrix products: 17 us -> none  [the longest x2 10.5 us: cross_block(): jnp.einsum('wkfi,wlfj->fkilj', own_bins, other_bins, preferred_element_ty...]
    ppermute x2 -> x11, waiting for transfers between devices: 89.8 us -> 75.5 us  [the longest x8 68.3 us: swap_blk(): lax.ppermute(piece, 'blk', [(i, i ^ stride) for i in range(lax.axis_size(...]
    convert_element_type x4 -> x0, other arithmetic: 7.71 us -> none  [the longest x2 5.09 us: cross_block(): return stacked.astype(jnp.bfloat16)]
    another operation x1, other arithmetic: 4.86 us -> 0.08 us  [body(): others = jnp.stack([mine ^ offset for offset in range(1, BANDS)])]
  transfers between devices with their start and end apart: 2 -> 11, of which waited for: 1 -> 6; matrix products, arithmetic and copies ran while one was open for 3% -> 0% of each run, Pallas kernels for 0% -> 6%
where the time goes in v1:
time: 126 us; the launch traced here: 125 us
  waiting for transfers between devices  75.5 us (60%)
  starting transfers between devices  25.9 us (21%)
  Pallas kernels  19.2 us (15%)
  local copies, waits for them, and re-layouts  4.12 us (3%)
    ppermute x8, waiting for transfers between devices, swap_blk(): lax.ppermute(piece, 'blk', [(i, i ^ stride) for i in range(lax.axis_size(...  68.3 us
    ppermute x8, starting transfers between devices, swap_blk(): lax.ppermute(piece, 'blk', [(i, i ^ stride) for i in range(lax.axis_size(...  22.4 us
    pallas_call x2, Pallas kernels, cross_blocks(): pl.pallas_call(functools.partial(cross_kernel, WINS * BANDS, bins), out_s...  9.76 us
    pallas_call x2, Pallas kernels, whiten_bands(): pl.pallas_call(functools.partial(spectra_kernel, parts), out_shape=[jax.S...  9.42 us
    ppermute x3, waiting for transfers between devices, swap_win(): lax.ppermute(piece, 'win', [(i, i ^ offset) for i in range(lax.axis_size(...  7.26 us
    unnamed x10, local copies, waits for them, and re-layouts  4.12 us
    ppermute x3, starting transfers between devices, swap_win(): lax.ppermute(piece, 'win', [(i, i ^ offset) for i in range(lax.axis_size(...  3.46 us
  transfers between devices with their start and end apart: 11, of which 6 were waited for; matrix products, arithmetic and copies ran while one was open for 0% of the time, Pallas kernels for 6%

profile of v1, /device:TPU:38, one launch (start us, length us, event | category | flops | bytes accessed | tf_op | source)
XLA Modules:
  0.0 125.5 jit_solution(2526465704255404976)
XLA Ops:
  0.6 0.1 pad_add_fusion.band_ref
  0.7 2.2 %copy-done = bf16[16,1024,128]{2,1,0:T(8,128)(2,1)S(1)} copy-done((bf16[16,1024,128]{2,1,0:T(8,128)(2,1)S(1)}, bf16[16,1024,128]{2,1,0:T(8,128)(2,1)}, u32[]{:S(2)}) %copy-start) | copy-done | bytes 4194328
  2.9 1.2 copy-done.2
  4.1 0.7 copy-done.4
  4.8 6.3 %shard_map.51 = (bf16[2048,128]{1,0:T(8,128)(2,1)S(1)}, bf16[2048,128]{1,0:T(8,128)(2,1)S(1)}, bf16[2048,128]{1,0:T(8,128)(2,1)S(1)}) custom-call(s32[3]{0:T(128)S(1)} %pad_add_fusion.band_ref, bf16[4,128,1024]{2,1,0:T(8,128)(2,1)S(1)} %copy-done.2, bf16[4,128,1024]{2,1,0:T(8,128)(2,1)S(1)} %copy-done.2, bf16[4,128,1024]{2,1,0:T(8,128)(2,1)S(1)} %copy-done.2, ...), custom_call_target="tpu_custom_call" | custom-call | flops 1610612736 | bytes 5767168 | tf_op jit(solution)/shard_map/pallas_call | solution.py:68
  11.1 0.1 collective-permute-start
  11.2 3.3 %collective-permute-start.1 = (bf16[2048,128]{1,0:T(8,128)(2,1)S(1)}, bf16[2048,128]{1,0:T(8,128)(2,1)S(1)}, u32[]{:S(2)}, u32[]{:S(2)}) collective-permute-start(bf16[2048,128]{1,0:T(8,128)(2,1)S(1)} %get-tuple-element.6), channel_id=1, source_target_pairs={{0,2},{1,3},{2,0},{3,1},{4,6},{5,7},{6,4},{7,5},{8,10},{9,11},{10,... | collective-permute-start | bytes 1572872 | tf_op jit(solution)/shard_map/ppermute | solution.py:128
  14.5 0.1 collective-permute-start.2
  14.6 0.0 copy-done.1
  14.6 0.0 copy-done.3
  14.6 3.2 %shard_map.50.refs_0_ = bf16[2048,128]{1,0:T(8,128)(2,1)S(1)} custom-call(s32[1]{0:T(128)} %bitcast.band_ref, bf16[4,128,1024]{2,1,0:T(8,128)(2,1)S(1)} %copy-done.3, bf16[16,1024,128]{2,1,0:T(8,128)(2,1)S(1)} %copy-done.1, s32[16,128]{1,0:T(8,128)S(1)} %copy-done.4), custom_call_target="tpu_custom_call" | custom-call | flops 536870912 | bytes 4718592 | tf_op jit(solution)/shard_map/pallas_call | solution.py:68
  17.7 6.4 %collective-permute-start.3 = (bf16[2048,128]{1,0:T(8,128)(2,1)S(1)}, bf16[2048,128]{1,0:T(8,128)(2,1)S(1)}, u32[]{:S(2)}, u32[]{:S(2)}) collective-permute-start(bf16[2048,128]{1,0:T(8,128)(2,1)S(1)} %shard_map.50.refs_0_), channel_id=1, source_target_pairs={{0,128},{4,132},{8,136},{12,140},{16,144},{20,148},{24,152},{28,15... | collective-permute-start | bytes 1572872 | tf_op jit(solution)/shard_map/ppermute | solution.py:132
  24.1 0.0 collective-permute-done.refs_1_
  24.1 0.1 collective-permute-start.4
  24.2 3.3 %collective-permute-done.1.refs_2_ = bf16[2048,128]{1,0:T(8,128)(2,1)S(1)} collective-permute-done((bf16[2048,128]{1,0:T(8,128)(2,1)S(1)}, bf16[2048,128]{1,0:T(8,128)(2,1)S(1)}, u32[]{:S(2)}, u32[]{:S(2)}) %collective-permute-start.1) | collective-permute-done | bytes 524320 | tf_op jit(solution)/shard_map/ppermute | solution.py:128
  27.5 6.3 %collective-permute-start.5 = (bf16[2048,128]{1,0:T(8,128)(2,1)S(1)}, bf16[2048,128]{1,0:T(8,128)(2,1)S(1)}, u32[]{:S(2)}, u32[]{:S(2)}) collective-permute-start(bf16[2048,128]{1,0:T(8,128)(2,1)S(1)} %collective-permute-done.1.refs_2_), channel_id=1, source_target_pairs={{0,128},{4,132},{8,136},{12,140},{16,144},{20,148},{24,152},{28,15... | collective-permute-start | bytes 1572872 | tf_op jit(solution)/shard_map/ppermute | solution.py:132
  33.8 4.0 %collective-permute-done.2.refs_3_ = bf16[2048,128]{1,0:T(8,128)(2,1)S(1)} collective-permute-done((bf16[2048,128]{1,0:T(8,128)(2,1)S(1)}, bf16[2048,128]{1,0:T(8,128)(2,1)S(1)}, u32[]{:S(2)}, u32[]{:S(2)}) %collective-permute-start.2) | collective-permute-done | bytes 524320 | tf_op jit(solution)/shard_map/ppermute | solution.py:128
  37.8 6.3 %collective-permute-start.6 = (bf16[2048,128]{1,0:T(8,128)(2,1)S(1)}, bf16[2048,128]{1,0:T(8,128)(2,1)S(1)}, u32[]{:S(2)}, u32[]{:S(2)}) collective-permute-start(bf16[2048,128]{1,0:T(8,128)(2,1)S(1)} %collective-permute-done.2.refs_3_), channel_id=1, source_target_pairs={{0,128},{4,132},{8,136},{12,140},{16,144},{20,148},{24,152},{28,15... | collective-permute-start | bytes 1572872 | tf_op jit(solution)/shard_map/ppermute | solution.py:132
  44.1 0.8 collective-permute-start.7
  44.9 7.5 %collective-permute-done.3.refs_4_ = bf16[2048,128]{1,0:T(8,128)(2,1)S(1)} collective-permute-done((bf16[2048,128]{1,0:T(8,128)(2,1)S(1)}, bf16[2048,128]{1,0:T(8,128)(2,1)S(1)}, u32[]{:S(2)}, u32[]{:S(2)}) %collective-permute-start.3) | collective-permute-done | bytes 524320 | tf_op jit(solution)/shard_map/ppermute | solution.py:132
  52.4 0.8 collective-permute-start.8
  53.3 25.2 %collective-permute-done.4.refs_5_ = bf16[2048,128]{1,0:T(8,128)(2,1)S(1)} collective-permute-done((bf16[2048,128]{1,0:T(8,128)(2,1)S(1)}, bf16[2048,128]{1,0:T(8,128)(2,1)S(1)}, u32[]{:S(2)}, u32[]{:S(2)}) %collective-permute-start.4) | collective-permute-done | bytes 524320 | tf_op jit(solution)/shard_map/ppermute | solution.py:132
  78.5 0.8 collective-permute-start.9
  79.3 21.4 %collective-permute-done.5.refs_6_ = bf16[2048,128]{1,0:T(8,128)(2,1)S(1)} collective-permute-done((bf16[2048,128]{1,0:T(8,128)(2,1)S(1)}, bf16[2048,128]{1,0:T(8,128)(2,1)S(1)}, u32[]{:S(2)}, u32[]{:S(2)}) %collective-permute-start.5) | collective-permute-done | bytes 524320 | tf_op jit(solution)/shard_map/ppermute | solution.py:132
  100.7 0.8 collective-permute-start.10
  101.5 14.2 %collective-permute-done.6.refs_7_ = bf16[2048,128]{1,0:T(8,128)(2,1)S(1)} collective-permute-done((bf16[2048,128]{1,0:T(8,128)(2,1)S(1)}, bf16[2048,128]{1,0:T(8,128)(2,1)S(1)}, u32[]{:S(2)}, u32[]{:S(2)}) %collective-permute-start.6) | collective-permute-done | bytes 524320 | tf_op jit(solution)/shard_map/ppermute | solution.py:132
  115.7 4.9 %shard_map.52 = bf16[64,2,128,128]{3,2,1,0:T(8,128)(2,1)} custom-call(bf16[2048,128]{1,0:T(8,128)(2,1)S(1)} %shard_map.50.refs_0_, bf16[2048,128]{1,0:T(8,128)(2,1)S(1)} %collective-permute-done.refs_1_, bf16[2048,128]{1,0:T(8,128)(2,1)S(1)} %collective-permute-done.1.refs_2_, bf16[2048,128]{1,0:T(8,128)(2,1)S(1)} %collective-permute-done.2.refs_3_, ...), custom_call_target="tpu_custom_call" | custom-call | flops 536870912 | bytes 8388608 | tf_op jit(solution)/shard_map/pallas_call | solution.py:112
  120.6 0.0 collective-permute-done.7.refs_4_
  120.6 0.0 collective-permute-done.8.refs_5_
  120.6 0.0 collective-permute-done.9.refs_6_
  120.6 0.0 collective-permute-done.10.refs_7_
  120.6 4.9 %shard_map.53 = bf16[64,2,128,128]{3,2,1,0:T(8,128)(2,1)} custom-call(bf16[2048,128]{1,0:T(8,128)(2,1)S(1)} %shard_map.50.refs_0_, bf16[2048,128]{1,0:T(8,128)(2,1)S(1)} %collective-permute-done.refs_1_, bf16[2048,128]{1,0:T(8,128)(2,1)S(1)} %collective-permute-done.1.refs_2_, bf16[2048,128]{1,0:T(8,128)(2,1)S(1)} %collective-permute-done.2.refs_3_, ...), custom_call_target="tpu_custom_call" | custom-call | flops 536870912 | bytes 8388608 | tf_op jit(solution)/shard_map/pallas_call | solution.py:112
  (5 shorter events, 0.0 us)
Async XLA Ops:
  0.7 2.2 %copy-start = (bf16[16,1024,128]{2,1,0:T(8,128)(2,1)S(1)}, bf16[16,1024,128]{2,1,0:T(8,128)(2,1)}, u32[]{:S(2)}) copy-start(bf16[16,1024,128]{2,1,0:T(8,128)(2,1)} %refs_3_.1) | copy-start | bytes 12582916
  2.9 1.2 copy-start.2
  4.1 0.7 copy-start.4
  4.8 9.7 %copy-start.1 = (bf16[16,1024,128]{2,1,0:T(8,128)(2,1)S(1)}, bf16[16,1024,128]{2,1,0:T(8,128)(2,1)}, u32[]{:S(2)}) copy-start(bf16[16,1024,128]{2,1,0:T(8,128)(2,1)} %refs_3_.1) | copy-start | bytes 12582916
  4.8 9.7 %copy-start.3 = (bf16[4,128,1024]{2,1,0:T(8,128)(2,1)S(1)}, bf16[4,128,1024]{2,1,0:T(8,128)(2,1)}, u32[]{:S(2)}) copy-start(bf16[4,128,1024]{2,1,0:T(8,128)(2,1)} %constant.12.clone.refs_0_.refs_1_.refs_2_) | copy-start | bytes 3145732
  11.1 13.0 %collective-permute-start = (bf16[2048,128]{1,0:T(8,128)(2,1)S(1)}, bf16[2048,128]{1,0:T(8,128)(2,1)S(1)}, u32[]{:S(2)}, u32[]{:S(2)}) collective-permute-start(bf16[2048,128]{1,0:T(8,128)(2,1)S(1)} %get-tuple-element.5), channel_id=1, source_target_pairs={{0,1},{1,0},{2,3},{3,2},{4,5},{5,4},{6,7},{7,6},{8,9},{9,8},{10,11... | collective-permute-start | bytes 1572872 | tf_op jit(solution)/shard_map/ppermute | solution.py:128
  11.2 16.3 %collective-permute-start.1 = (bf16[2048,128]{1,0:T(8,128)(2,1)S(1)}, bf16[2048,128]{1,0:T(8,128)(2,1)S(1)}, u32[]{:S(2)}, u32[]{:S(2)}) collective-permute-start(bf16[2048,128]{1,0:T(8,128)(2,1)S(1)} %get-tuple-element.6), channel_id=1, source_target_pairs={{0,2},{1,3},{2,0},{3,1},{4,6},{5,7},{6,4},{7,5},{8,10},{9,11},{10,... | collective-permute-start | bytes 1572872 | tf_op jit(solution)/shard_map/ppermute | solution.py:128
  14.5 23.3 %collective-permute-start.2 = (bf16[2048,128]{1,0:T(8,128)(2,1)S(1)}, bf16[2048,128]{1,0:T(8,128)(2,1)S(1)}, u32[]{:S(2)}, u32[]{:S(2)}) collective-permute-start(bf16[2048,128]{1,0:T(8,128)(2,1)S(1)} %get-tuple-element.7), channel_id=1, source_target_pairs={{0,3},{1,2},{2,1},{3,0},{4,7},{5,6},{6,5},{7,4},{8,11},{9,10},{10,... | collective-permute-start | bytes 1572872 | tf_op jit(solution)/shard_map/ppermute | solution.py:128
  17.7 34.7 %collective-permute-start.3 = (bf16[2048,128]{1,0:T(8,128)(2,1)S(1)}, bf16[2048,128]{1,0:T(8,128)(2,1)S(1)}, u32[]{:S(2)}, u32[]{:S(2)}) collective-permute-start(bf16[2048,128]{1,0:T(8,128)(2,1)S(1)} %shard_map.50.refs_0_), channel_id=1, source_target_pairs={{0,128},{4,132},{8,136},{12,140},{16,144},{20,148},{24,152},{28,15... | collective-permute-start | bytes 1572872 | tf_op jit(solution)/shard_map/ppermute | solution.py:132
  24.1 54.3 %collective-permute-start.4 = (bf16[2048,128]{1,0:T(8,128)(2,1)S(1)}, bf16[2048,128]{1,0:T(8,128)(2,1)S(1)}, u32[]{:S(2)}, u32[]{:S(2)}) collective-permute-start(bf16[2048,128]{1,0:T(8,128)(2,1)S(1)} %collective-permute-done.refs_1_), channel_id=1, source_target_pairs={{0,128},{4,132},{8,136},{12,140},{16,144},{20,148},{24,152},{28,15... | collective-permute-start | bytes 1572872 | tf_op jit(solution)/shard_map/ppermute | solution.py:132
  27.5 73.2 %collective-permute-start.5 = (bf16[2048,128]{1,0:T(8,128)(2,1)S(1)}, bf16[2048,128]{1,0:T(8,128)(2,1)S(1)}, u32[]{:S(2)}, u32[]{:S(2)}) collective-permute-start(bf16[2048,128]{1,0:T(8,128)(2,1)S(1)} %collective-permute-done.1.refs_2_), channel_id=1, source_target_pairs={{0,128},{4,132},{8,136},{12,140},{16,144},{20,148},{24,152},{28,15... | collective-permute-start | bytes 1572872 | tf_op jit(solution)/shard_map/ppermute | solution.py:132
  37.8 77.9 %collective-permute-start.6 = (bf16[2048,128]{1,0:T(8,128)(2,1)S(1)}, bf16[2048,128]{1,0:T(8,128)(2,1)S(1)}, u32[]{:S(2)}, u32[]{:S(2)}) collective-permute-start(bf16[2048,128]{1,0:T(8,128)(2,1)S(1)} %collective-permute-done.2.refs_3_), channel_id=1, source_target_pairs={{0,128},{4,132},{8,136},{12,140},{16,144},{20,148},{24,152},{28,15... | collective-permute-start | bytes 1572872 | tf_op jit(solution)/shard_map/ppermute | solution.py:132
  44.1 76.5 %collective-permute-start.7 = (bf16[2048,128]{1,0:T(8,128)(2,1)S(1)}, bf16[2048,128]{1,0:T(8,128)(2,1)S(1)}, u32[]{:S(2)}, u32[]{:S(2)}) collective-permute-start(bf16[2048,128]{1,0:T(8,128)(2,1)S(1)} %shard_map.50.refs_0_), channel_id=1, source_target_pairs={{0,4},{4,0},{8,12},{12,8},{16,20},{20,16},{24,28},{28,24},{32,36},... | collective-permute-start | bytes 1572872 | tf_op jit(solution)/shard_map/ppermute | solution.py:132
  52.4 68.1 %collective-permute-start.8 = (bf16[2048,128]{1,0:T(8,128)(2,1)S(1)}, bf16[2048,128]{1,0:T(8,128)(2,1)S(1)}, u32[]{:S(2)}, u32[]{:S(2)}) collective-permute-start(bf16[2048,128]{1,0:T(8,128)(2,1)S(1)} %collective-permute-done.refs_1_), channel_id=1, source_target_pairs={{0,4},{4,0},{8,12},{12,8},{16,20},{20,16},{24,28},{28,24},{32,36},... | collective-permute-start | bytes 1572872 | tf_op jit(solution)/shard_map/ppermute | solution.py:132
  78.5 42.1 %collective-permute-start.9 = (bf16[2048,128]{1,0:T(8,128)(2,1)S(1)}, bf16[2048,128]{1,0:T(8,128)(2,1)S(1)}, u32[]{:S(2)}, u32[]{:S(2)}) collective-permute-start(bf16[2048,128]{1,0:T(8,128)(2,1)S(1)} %collective-permute-done.1.refs_2_), channel_id=1, source_target_pairs={{0,4},{4,0},{8,12},{12,8},{16,20},{20,16},{24,28},{28,24},{32,36},... | collective-permute-start | bytes 1572872 | tf_op jit(solution)/shard_map/ppermute | solution.py:132
  100.7 19.9 %collective-permute-start.10 = (bf16[2048,128]{1,0:T(8,128)(2,1)S(1)}, bf16[2048,128]{1,0:T(8,128)(2,1)S(1)}, u32[]{:S(2)}, u32[]{:S(2)}) collective-permute-start(bf16[2048,128]{1,0:T(8,128)(2,1)S(1)} %collective-permute-done.2.refs_3_), channel_id=1, source_target_pairs={{0,4},{4,0},{8,12},{12,8},{16,20},{20,16},{24,28},{28,24},{32,36},... | collective-permute-start | bytes 1572872 | tf_op jit(solution)/shard_map/ppermute | solution.py:132

commit v2 on v1

v2 whole, which is shorter than its diff:
```python
import functools
import math

import jax
import jax.numpy as jnp
import ml_dtypes
import numpy as np
from jax import lax
from jax.experimental import pallas as pl
from jax.experimental.pallas import tpu as pltpu
from jax.sharding import PartitionSpec as P

BINS = 256
SAMPLES = 1024
LOW = 32
BAND = 64
BANDS = BINS // BAND
CH = 128
WINS = 16
ROWS = 2 * WINS
PITCH = 40
PAIR = 2
GROUP = 8
STEP = 8
HEAD = 48
VMEM_LIMIT = 48 * 1024 * 1024
SPECTRA_VMEM = 62 * 1024 * 1024


def band_twiddles():
    sample_index = np.arange(SAMPLES, dtype=np.int32)
    bin_index = LOW + np.arange(BINS, dtype=np.int32)
    phase_step = bin_index[:, None] * sample_index[None, :] % SAMPLES
    angles = phase_step.astype(np.float32) * np.float32(2.0 * math.pi / SAMPLES)
    table = np.stack(
        [np.cos(angles).reshape(BANDS, BAND, SAMPLES), -np.sin(angles).reshape(BANDS, BAND, SAMPLES)],
        axis=1,
    )
    return table.reshape(BANDS, 2 * BAND, SAMPLES).astype(ml_dtypes.bfloat16)


def spectra_kernel(offsets, outs, table_ref, raw_ref, mask_ref, *refs):
    parts = len(offsets)
    out_refs, refs = refs[: len(outs)], refs[len(outs) :]
    twiddle, raw, mask = refs[:3]
    wide_refs = refs[3 : parts + 3]
    twiddle_sems, raw_sems, mask_sem = refs[parts + 3 :]
    mine = lax.axis_index("win")
    mask_copy = pltpu.make_async_copy(mask_ref, mask, mask_sem)
    twiddle_copies = [
        pltpu.make_async_copy(
            table_ref.at[lax.bitwise_xor(mine, jnp.int32(offset))], twiddle.at[part], twiddle_sems.at[part]
        )
        for part, offset in enumerate(offsets)
    ]
    raw_copies = [
        pltpu.make_async_copy(
            raw_ref.at[pl.ds(group * GROUP, GROUP)], raw.at[pl.ds(group * GROUP, GROUP)], raw_sems.at[group]
        )
        for group in range(WINS // GROUP)
    ]
    for copy in [mask_copy] + twiddle_copies + raw_copies:
        copy.start()
    for copy in [mask_copy] + twiddle_copies:
        copy.wait()
    left = twiddle[...].reshape(parts * 2 * BAND, SAMPLES)
    for group in range(WINS // GROUP):
        raw_copies[group].wait()
        for first in range(group * GROUP, (group + 1) * GROUP, PAIR):
            pair = jnp.concatenate([raw[first], raw[first + 1]], axis=1)
            spectra = jnp.dot(left, pair, preferred_element_type=jnp.float32)
            for part in range(parts):
                real = spectra[part * 2 * BAND : (part * 2 + 1) * BAND]
                imag = spectra[(part * 2 + 1) * BAND : (part * 2 + 2) * BAND]
                power = jnp.sum(real * real + imag * imag, axis=0, keepdims=True) * (1.0 / BAND)
                scale = lax.rsqrt(power + 1e-06)
                for half in range(PAIR):
                    window = first + half
                    cols = slice(half * CH, (half + 1) * CH)
                    weight = scale[:, cols] * mask[window : window + 1, :].astype(jnp.float32)
                    wide = wide_refs[part]
                    wide[pl.ds(window, BAND, stride=PITCH), :] = real[:, cols] * weight
                    wide[pl.ds(window + WINS, BAND, stride=PITCH), :] = imag[:, cols] * weight
    for out_ref, (part, start, stop) in zip(out_refs, outs):
        for bin_index in range(start, stop):
            out_ref[(bin_index - start) * ROWS : (bin_index - start + 1) * ROWS, :] = wide_refs[part][
                bin_index * PITCH : bin_index * PITCH + ROWS, :
            ].astype(jnp.bfloat16)


def whiten_bands(offsets, outs, table, raw_traces, channel_mask):
    parts = len(offsets)
    anywhere = pl.BlockSpec(memory_space=pltpu.HBM)
    return pl.pallas_call(
        functools.partial(spectra_kernel, offsets, outs),
        out_shape=[
            jax.ShapeDtypeStruct(((stop - start) * ROWS, CH), jnp.bfloat16) for _, start, stop in outs
        ],
        in_specs=[anywhere] * 3,
        out_specs=[pl.BlockSpec(memory_space=pltpu.VMEM)] * len(outs),
        scratch_shapes=[
            pltpu.VMEM((parts, 2 * BAND, SAMPLES), jnp.bfloat16),
            pltpu.VMEM((WINS, SAMPLES, CH), jnp.bfloat16),
            pltpu.VMEM((WINS, CH), jnp.int32),
        ]
        + [pltpu.VMEM((BAND * PITCH, CH), jnp.float32)] * parts
        + [
            pltpu.SemaphoreType.DMA((parts,)),
            pltpu.SemaphoreType.DMA((WINS // GROUP,)),
            pltpu.SemaphoreType.DMA(()),
        ],
        compiler_params=pltpu.CompilerParams(vmem_limit_bytes=SPECTRA_VMEM),
        cost_estimate=pl.CostEstimate(
            flops=2 * WINS * CH * SAMPLES * 2 * BAND * parts,
            bytes_accessed=2 * WINS * CH * SAMPLES + parts * 2 * BAND * ROWS * CH,
            transcendentals=0,
        ),
    )(table, raw_traces, channel_mask)


def cross_kernel(bins, *refs):
    own_refs, other_refs, out_ref = refs[:BANDS], refs[BANDS : 2 * BANDS], refs[-1]
    scale = 1.0 / math.sqrt(WINS * BANDS)
    for index in range(bins):
        rows = slice(index * ROWS, (index + 1) * ROWS)
        own = [ref[rows, :] for ref in own_refs]
        turned = []
        for piece in own:
            turned += [piece[WINS:], -piece[:WINS]]
        left = jnp.concatenate([jnp.concatenate(own, axis=0), jnp.concatenate(turned, axis=0)], axis=1)
        right = jnp.concatenate([ref[rows, :] for ref in other_refs], axis=0)
        tile = lax.dot_general(left, right, (((0,), (0,)), ((), ())), preferred_element_type=jnp.float32)
        tile = (tile * scale).astype(jnp.bfloat16)
        out_ref[index, 0] = tile[:CH]
        out_ref[index, 1] = tile[CH:]


def cross_blocks(own, other, first, last, into=None):
    bins = STEP
    steps = (last - first) // bins

    def piece(start):
        return pl.BlockSpec((bins * ROWS, CH), lambda step: ((first - start) // bins + step, 0))

    arrays = list(own) + [array for array, _ in other]
    in_specs = [piece(0)] * BANDS + [piece(start) for _, start in other]
    aliases = {}
    if into is not None:
        aliases = {len(arrays): 0}
        arrays.append(into)
        in_specs.append(pl.BlockSpec(memory_space=pl.ANY))
    return pl.pallas_call(
        functools.partial(cross_kernel, bins),
        out_shape=jax.ShapeDtypeStruct((BAND, 2, CH, CH), jnp.bfloat16),
        grid=(steps,),
        in_specs=in_specs,
        out_specs=pl.BlockSpec((bins, 2, CH, CH), lambda step: (first // bins + step, 0, 0, 0)),
        input_output_aliases=aliases,
        compiler_params=pltpu.CompilerParams(vmem_limit_bytes=VMEM_LIMIT),
        cost_estimate=pl.CostEstimate(
            flops=2 * (last - first) * 2 * CH * CH * 2 * WINS * BANDS,
            bytes_accessed=(last - first) * (4 * CH * CH + 4 * BANDS * ROWS * CH),
            transcendentals=0,
        ),
    )(*arrays)


def swap_win(piece, offset):
    return lax.ppermute(piece, "win", [(i, i ^ offset) for i in range(lax.axis_size("win"))])


def swap_blk(piece, stride):
    return lax.ppermute(piece, "blk", [(i, i ^ stride) for i in range(lax.axis_size("blk"))])


def tie(*arrays):
    return lax.optimization_barrier(arrays)


def body(raw_traces, channel_mask):
    table = jnp.asarray(band_twiddles())
    far = lax.axis_size("blk") // 2
    split = HEAD * ROWS
    pieces = tuple((part, 0, BAND) for part in range(BANDS))
    own0, leaving1, leaving2, leaving3 = whiten_bands(tuple(range(BANDS)), pieces, table, raw_traces, channel_mask)
    far0 = swap_blk(own0, far)
    own3, own2, own1 = swap_win(leaving3, 3), swap_win(leaving2, 2), swap_win(leaving1, 1)
    head = jnp.concatenate([own2[:split], own3[:split]])
    tail = jnp.concatenate([own2[split:], own3[split:]])
    near0 = swap_blk(own0, 1)
    far1 = swap_blk(own1, far)
    own1_next, far0, near0 = tie(own1, far0, near0)
    near1 = swap_blk(own1_next, 1)
    near23 = swap_blk(jnp.concatenate([own2, own3]), 1)
    far_head, far_tail = swap_blk(head, far), swap_blk(tail, far)
    own = (own0, own1, own2, own3)
    far_pieces = [(far0, 0), (far1, 0)]
    second = cross_blocks(own, [(near0, 0), (near1, 0), (near23, 0), (near23, -BAND)], 0, BAND)
    far_head, second = tie(far_head, second)
    first = cross_blocks(own, far_pieces + [(far_head, 0), (far_head, -HEAD)], 0, HEAD)
    first = cross_blocks(own, far_pieces + [(far_tail, HEAD), (far_tail, 2 * HEAD - BAND)], HEAD, BAND, first)
    return first, second


def solution(mesh):
    in_specs = (P("win", None, "blk"), P("win", "blk"))
    out_specs = (P("win", None, "blk", None), P("win", None, "blk", None))
    return jax.shard_map(body, mesh=mesh, in_specs=in_specs, out_specs=out_specs, check_vma=False)
```

time: 126 us -> 117 us (0.929)
  the two profiles are of different devices: /device:TPU:38 before, /device:TPU:1 now
where the time goes in v2:
time: 117 us
  waiting for transfers between devices  71.9 us (61%)
  starting transfers between devices  27.6 us (24%)
  Pallas kernels  16.7 us (14%)
    ppermute x7, waiting for transfers between devices, swap_blk(): lax.ppermute(piece, 'blk', [(i, i ^ stride) for i in range(lax.axis_size(...  57.6 us
    ppermute x7, starting transfers between devices, swap_blk(): lax.ppermute(piece, 'blk', [(i, i ^ stride) for i in range(lax.axis_size(...  20.6 us
    ppermute x3, waiting for transfers between devices, swap_win(): lax.ppermute(piece, 'win', [(i, i ^ offset) for i in range(lax.axis_size(...  14.3 us
    pallas_call x3, Pallas kernels, cross_blocks(): pl.pallas_call(functools.partial(cross_kernel, bins), out_shape=jax.Shape...  10.1 us
    ppermute x3, starting transfers between devices, swap_win(): lax.ppermute(piece, 'win', [(i, i ^ offset) for i in range(lax.axis_size(...  7.08 us
    pallas_call x1, Pallas kernels, whiten_bands(): pl.pallas_call(functools.partial(spectra_kernel, offsets, outs), out_shap...  6.61 us
  transfers between devices with their start and end apart: 10, of which 6 were waited for; matrix products, arithmetic and copies ran while one was open for 0% of the time, Pallas kernels for 7%

profile of v2, /device:TPU:1, one launch (start us, length us, event | category | flops | bytes accessed | tf_op | source)
XLA Modules:
  0.0 117.2 jit_solution(5986375519095921133)
XLA Ops:
  0.6 6.6 %shard_map.50 = (bf16[2048,128]{1,0:T(8,128)(2,1)}, bf16[2048,128]{1,0:T(8,128)(2,1)}, bf16[2048,128]{1,0:T(8,128)(2,1)}, bf16[2048,128]{1,0:T(8,128)(2,1)}) custom-call(bf16[4,128,1024]{2,1,0:T(8,128)(2,1)} %constant.2.clone.table_ref, bf16[16,1024,128]{2,1,0:T(8,128)(2,1)} %raw_ref.1, s32[16,128]{1,0:T(8,128)} %mask_ref.1), custom_call_target="tpu_custom_call" | custom-call | flops 2147483648 | bytes 6291456 | tf_op jit(solution)/shard_map/pallas_call | solution.py:94
  7.3 3.8 %collective-permute-start.1 = (bf16[2048,128]{1,0:T(8,128)(2,1)}, bf16[2048,128]{1,0:T(8,128)(2,1)S(1)}, u32[]{:S(2)}, u32[]{:S(2)}) collective-permute-start(bf16[2048,128]{1,0:T(8,128)(2,1)} %get-tuple-element.13), channel_id=1, source_target_pairs={{0,2},{1,3},{2,0},{3,1},{4,6},{5,7},{6,4},{7,5},{8,10},{9,11},{10,... | collective-permute-start | bytes 1572872 | tf_op jit(solution)/shard_map/ppermute | solution.py:169
  11.1 2.6 %collective-permute-start.2 = (bf16[2048,128]{1,0:T(8,128)(2,1)}, bf16[2048,128]{1,0:T(8,128)(2,1)S(1)}, u32[]{:S(2)}, u32[]{:S(2)}) collective-permute-start(bf16[2048,128]{1,0:T(8,128)(2,1)} %get-tuple-element.14), channel_id=1, source_target_pairs={{0,3},{1,2},{2,1},{3,0},{4,7},{5,6},{6,5},{7,4},{8,11},{9,10},{10,... | collective-permute-start | bytes 1572872 | tf_op jit(solution)/shard_map/ppermute | solution.py:169
  13.7 0.0 collective-permute-start.4
  13.7 6.4 %collective-permute-start.3 = (bf16[2048,128]{1,0:T(8,128)(2,1)}, bf16[2048,128]{1,0:T(8,128)(2,1)S(1)}, u32[]{:S(2)}, u32[]{:S(2)}) collective-permute-start(bf16[2048,128]{1,0:T(8,128)(2,1)} %get-tuple-element.11.refs_0_), channel_id=1, source_target_pairs={{0,128},{4,132},{8,136},{12,140},{16,144},{20,148},{24,152},{28,15... | collective-permute-start | bytes 1572872 | tf_op jit(solution)/shard_map/ppermute | solution.py:173
  20.1 0.6 collective-permute-start
  20.7 1.3 %collective-permute-done.1.refs_2_ = bf16[2048,128]{1,0:T(8,128)(2,1)S(1)} collective-permute-done((bf16[2048,128]{1,0:T(8,128)(2,1)}, bf16[2048,128]{1,0:T(8,128)(2,1)S(1)}, u32[]{:S(2)}, u32[]{:S(2)}) %collective-permute-start.1) | collective-permute-done | bytes 524320 | tf_op jit(solution)/shard_map/ppermute | solution.py:169
  22.0 13.0 %collective-permute-done.2.refs_3_ = bf16[2048,128]{1,0:T(8,128)(2,1)S(1)} collective-permute-done((bf16[2048,128]{1,0:T(8,128)(2,1)}, bf16[2048,128]{1,0:T(8,128)(2,1)S(1)}, u32[]{:S(2)}, u32[]{:S(2)}) %collective-permute-start.2) | collective-permute-done | bytes 524320 | tf_op jit(solution)/shard_map/ppermute | solution.py:169
  35.0 0.1 pad_maximum_fusion
  35.1 0.0 copy-start
  35.1 1.1 collective-permute-start.9
  36.2 0.1 pad_maximum_fusion.1
  36.3 7.0 %collective-permute-start.7 = (bf16[3072,128]{1,0:T(8,128)(2,1)S(1)}, bf16[3072,128]{1,0:T(8,128)(2,1)S(1)}, u32[]{:S(2)}, u32[]{:S(2)}) collective-permute-start(bf16[3072,128]{1,0:T(8,128)(2,1)S(1)} %pad_maximum_fusion.1), channel_id=1, source_target_pairs={{0,128},{4,132},{8,136},{12,140},{16,144},{20,148},{24,152},{28,15... | collective-permute-start | bytes 2359304 | tf_op jit(solution)/shard_map/ppermute | solution.py:173
  43.3 0.0 collective-permute-done.refs_1_
  43.3 0.0 collective-permute-done.4.refs_4_
  43.3 0.0 collective-permute-done.3.refs_4_
  43.3 0.6 collective-permute-start.8
  43.9 0.0 collective-permute-start.5
  44.0 5.4 %collective-permute-start.6 = (bf16[1024,128]{1,0:T(8,128)(2,1)S(1)}, bf16[1024,128]{1,0:T(8,128)(2,1)S(1)}, u32[]{:S(2)}, u32[]{:S(2)}) collective-permute-start(bf16[1024,128]{1,0:T(8,128)(2,1)S(1)} %pad_maximum_fusion.2), channel_id=1, source_target_pairs={{0,128},{4,132},{8,136},{12,140},{16,144},{20,148},{24,152},{28,15... | collective-permute-start | bytes 786440 | tf_op jit(solution)/shard_map/ppermute | solution.py:173
  49.4 21.9 %collective-permute-done.8.refs_5_ = bf16[2048,128]{1,0:T(8,128)(2,1)S(1)} collective-permute-done((bf16[2048,128]{1,0:T(8,128)(2,1)S(1)}, bf16[2048,128]{1,0:T(8,128)(2,1)S(1)}, u32[]{:S(2)}, u32[]{:S(2)}) %collective-permute-start.8) | collective-permute-done | bytes 524320 | tf_op jit(solution)/shard_map/ppermute | solution.py:173
  71.3 0.0 collective-permute-done.9.refs_6_.refs_7_
  71.3 0.0 copy-done
  71.3 4.9 %shard_map.51 = bf16[64,2,128,128]{3,2,1,0:T(8,128)(2,1)} custom-call(bf16[2048,128]{1,0:T(8,128)(2,1)S(1)} %copy-done, bf16[2048,128]{1,0:T(8,128)(2,1)S(1)} %collective-permute-done.refs_1_, bf16[2048,128]{1,0:T(8,128)(2,1)S(1)} %collective-permute-done.1.refs_2_, bf16[2048,128]{1,0:T(8,128)(2,1)S(1)} %collective-permute-done.2.refs_3_, ...), custom_call_target="tpu_custom_call" | custom-call | flops 536870912 | bytes 8388608 | tf_op jit(solution)/shard_map/pallas_call | solution.py:152
  76.2 22.6 %collective-permute-done.7.refs_6_.refs_7_ = bf16[3072,128]{1,0:T(8,128)(2,1)S(1)} collective-permute-done((bf16[3072,128]{1,0:T(8,128)(2,1)S(1)}, bf16[3072,128]{1,0:T(8,128)(2,1)S(1)}, u32[]{:S(2)}, u32[]{:S(2)}) %collective-permute-start.7) | collective-permute-done | bytes 786464 | tf_op jit(solution)/shard_map/ppermute | solution.py:173
  98.8 11.2 %collective-permute-done.5.refs_5_ = bf16[2048,128]{1,0:T(8,128)(2,1)S(1)} collective-permute-done((bf16[2048,128]{1,0:T(8,128)(2,1)S(1)}, bf16[2048,128]{1,0:T(8,128)(2,1)S(1)}, u32[]{:S(2)}, u32[]{:S(2)}) %collective-permute-start.5) | collective-permute-done | bytes 524320 | tf_op jit(solution)/shard_map/ppermute | solution.py:173
  110.1 3.7 %shard_map.52.refs_8_ = bf16[64,2,128,128]{3,2,1,0:T(8,128)(2,1)} custom-call(bf16[2048,128]{1,0:T(8,128)(2,1)S(1)} %copy-done, bf16[2048,128]{1,0:T(8,128)(2,1)S(1)} %collective-permute-done.refs_1_, bf16[2048,128]{1,0:T(8,128)(2,1)S(1)} %collective-permute-done.1.refs_2_, bf16[2048,128]{1,0:T(8,128)(2,1)S(1)} %collective-permute-done.2.refs_3_, ...), custom_call_target="tpu_custom_call" | custom-call | flops 402653184 | bytes 6291456 | tf_op jit(solution)/shard_map/pallas_call | solution.py:152
  113.8 1.9 %collective-permute-done.6.refs_6_.refs_7_ = bf16[1024,128]{1,0:T(8,128)(2,1)S(1)} collective-permute-done((bf16[1024,128]{1,0:T(8,128)(2,1)S(1)}, bf16[1024,128]{1,0:T(8,128)(2,1)S(1)}, u32[]{:S(2)}, u32[]{:S(2)}) %collective-permute-start.6) | collective-permute-done | bytes 262176 | tf_op jit(solution)/shard_map/ppermute | solution.py:173
  115.7 1.5 %shard_map.53 = bf16[64,2,128,128]{3,2,1,0:T(8,128)(2,1)} custom-call(bf16[2048,128]{1,0:T(8,128)(2,1)S(1)} %copy-done, bf16[2048,128]{1,0:T(8,128)(2,1)S(1)} %collective-permute-done.refs_1_, bf16[2048,128]{1,0:T(8,128)(2,1)S(1)} %collective-permute-done.1.refs_2_, ...), custom_call_target="tpu_custom_call", output_to_operand_aliasing={{}: (8, {})} | custom-call | flops 134217728 | bytes 2097152 | tf_op jit(solution)/shard_map/pallas_call | solution.py:152
  (5 shorter events, 0.1 us)
Async XLA Ops:
  7.3 14.8 %collective-permute-start.1 = (bf16[2048,128]{1,0:T(8,128)(2,1)}, bf16[2048,128]{1,0:T(8,128)(2,1)S(1)}, u32[]{:S(2)}, u32[]{:S(2)}) collective-permute-start(bf16[2048,128]{1,0:T(8,128)(2,1)} %get-tuple-element.13), channel_id=1, source_target_pairs={{0,2},{1,3},{2,0},{3,1},{4,6},{5,7},{6,4},{7,5},{8,10},{9,11},{10,... | collective-permute-start | bytes 1572872 | tf_op jit(solution)/shard_map/ppermute | solution.py:169
  11.1 23.9 %collective-permute-start.2 = (bf16[2048,128]{1,0:T(8,128)(2,1)}, bf16[2048,128]{1,0:T(8,128)(2,1)S(1)}, u32[]{:S(2)}, u32[]{:S(2)}) collective-permute-start(bf16[2048,128]{1,0:T(8,128)(2,1)} %get-tuple-element.14), channel_id=1, source_target_pairs={{0,3},{1,2},{2,1},{3,0},{4,7},{5,6},{6,5},{7,4},{8,11},{9,10},{10,... | collective-permute-start | bytes 1572872 | tf_op jit(solution)/shard_map/ppermute | solution.py:169
  13.7 29.6 %collective-permute-start.4 = (bf16[2048,128]{1,0:T(8,128)(2,1)}, bf16[2048,128]{1,0:T(8,128)(2,1)S(1)}, u32[]{:S(2)}, u32[]{:S(2)}) collective-permute-start(bf16[2048,128]{1,0:T(8,128)(2,1)} %get-tuple-element.11.refs_0_), channel_id=1, source_target_pairs={{0,4},{4,0},{8,12},{12,8},{16,20},{20,16},{24,28},{28,24},{32,36},... | collective-permute-start | bytes 1572872 | tf_op jit(solution)/shard_map/ppermute | solution.py:173
  13.7 29.6 %collective-permute-start.3 = (bf16[2048,128]{1,0:T(8,128)(2,1)}, bf16[2048,128]{1,0:T(8,128)(2,1)S(1)}, u32[]{:S(2)}, u32[]{:S(2)}) collective-permute-start(bf16[2048,128]{1,0:T(8,128)(2,1)} %get-tuple-element.11.refs_0_), channel_id=1, source_target_pairs={{0,128},{4,132},{8,136},{12,140},{16,144},{20,148},{24,152},{28,15... | collective-permute-start | bytes 1572872 | tf_op jit(solution)/shard_map/ppermute | solution.py:173
  20.1 23.2 %collective-permute-start = (bf16[2048,128]{1,0:T(8,128)(2,1)}, bf16[2048,128]{1,0:T(8,128)(2,1)S(1)}, u32[]{:S(2)}, u32[]{:S(2)}) collective-permute-start(bf16[2048,128]{1,0:T(8,128)(2,1)} %get-tuple-element.12), channel_id=1, source_target_pairs={{0,1},{1,0},{2,3},{3,2},{4,5},{5,4},{6,7},{7,6},{8,9},{9,8},{10,11... | collective-permute-start | bytes 1572872 | tf_op jit(solution)/shard_map/ppermute | solution.py:169
  35.1 36.3 %copy-start = (bf16[2048,128]{1,0:T(8,128)(2,1)S(1)}, bf16[2048,128]{1,0:T(8,128)(2,1)}, u32[]{:S(2)}) copy-start(bf16[2048,128]{1,0:T(8,128)(2,1)} %get-tuple-element.11.refs_0_) | copy-start | bytes 1572868
  35.1 36.2 %collective-permute-start.9 = (bf16[4096,128]{1,0:T(8,128)(2,1)S(1)}, bf16[4096,128]{1,0:T(8,128)(2,1)S(1)}, u32[]{:S(2)}, u32[]{:S(2)}) collective-permute-start(bf16[4096,128]{1,0:T(8,128)(2,1)S(1)} %pad_maximum_fusion), channel_id=1, source_target_pairs={{0,4},{4,0},{8,12},{12,8},{16,20},{20,16},{24,28},{28,24},{32,36},... | collective-permute-start | bytes 3145736 | tf_op jit(solution)/shard_map/ppermute | solution.py:173
  36.3 62.5 %collective-permute-start.7 = (bf16[3072,128]{1,0:T(8,128)(2,1)S(1)}, bf16[3072,128]{1,0:T(8,128)(2,1)S(1)}, u32[]{:S(2)}, u32[]{:S(2)}) collective-permute-start(bf16[3072,128]{1,0:T(8,128)(2,1)S(1)} %pad_maximum_fusion.1), channel_id=1, source_target_pairs={{0,128},{4,132},{8,136},{12,140},{16,144},{20,148},{24,152},{28,15... | collective-permute-start | bytes 2359304 | tf_op jit(solution)/shard_map/ppermute | solution.py:173
  43.3 28.0 %collective-permute-start.8 = (bf16[2048,128]{1,0:T(8,128)(2,1)S(1)}, bf16[2048,128]{1,0:T(8,128)(2,1)S(1)}, u32[]{:S(2)}, u32[]{:S(2)}) collective-permute-start(bf16[2048,128]{1,0:T(8,128)(2,1)S(1)} %collective-permute-done.refs_1_), channel_id=1, source_target_pairs={{0,4},{4,0},{8,12},{12,8},{16,20},{20,16},{24,28},{28,24},{32,36},... | collective-permute-start | bytes 1572872 | tf_op jit(solution)/shard_map/ppermute | solution.py:173
  43.9 66.1 %collective-permute-start.5 = (bf16[2048,128]{1,0:T(8,128)(2,1)S(1)}, bf16[2048,128]{1,0:T(8,128)(2,1)S(1)}, u32[]{:S(2)}, u32[]{:S(2)}) collective-permute-start(bf16[2048,128]{1,0:T(8,128)(2,1)S(1)} %collective-permute-done.refs_1_), channel_id=1, source_target_pairs={{0,128},{4,132},{8,136},{12,140},{16,144},{20,148},{24,152},{28,15... | collective-permute-start | bytes 1572872 | tf_op jit(solution)/shard_map/ppermute | solution.py:173
  44.0 71.7 %collective-permute-start.6 = (bf16[1024,128]{1,0:T(8,128)(2,1)S(1)}, bf16[1024,128]{1,0:T(8,128)(2,1)S(1)}, u32[]{:S(2)}, u32[]{:S(2)}) collective-permute-start(bf16[1024,128]{1,0:T(8,128)(2,1)S(1)} %pad_maximum_fusion.2), channel_id=1, source_target_pairs={{0,128},{4,132},{8,136},{12,140},{16,144},{20,148},{24,152},{28,15... | collective-permute-start | bytes 786440 | tf_op jit(solution)/shard_map/ppermute | solution.py:173

commit v3 on v2

--- a/solution.py
+++ b/solution.py
@@ -21,9 +21,8 @@
 PITCH = 40
 PAIR = 2
 GROUP = 8
-STEP = 8
-HEAD = 48
-VMEM_LIMIT = 48 * 1024 * 1024
+CHUNK = 8
+VMEM_LIMIT = 32 * 1024 * 1024
 SPECTRA_VMEM = 62 * 1024 * 1024
 
 
@@ -81,11 +80,13 @@
                     wide = wide_refs[part]
                     wide[pl.ds(window, BAND, stride=PITCH), :] = real[:, cols] * weight
                     wide[pl.ds(window + WINS, BAND, stride=PITCH), :] = imag[:, cols] * weight
-    for out_ref, (part, start, stop) in zip(out_refs, outs):
-        for bin_index in range(start, stop):
-            out_ref[(bin_index - start) * ROWS : (bin_index - start + 1) * ROWS, :] = wide_refs[part][
-                bin_index * PITCH : bin_index * PITCH + ROWS, :
-            ].astype(jnp.bfloat16)
+    for out_ref, runs in zip(out_refs, outs):
+        for place, part in enumerate(runs):
+            for bin_index in range(BAND):
+                row = (place * BAND + bin_index) * ROWS
+                out_ref[row : row + ROWS, :] = wide_refs[part][
+                    bin_index * PITCH : bin_index * PITCH + ROWS, :
+                ].astype(jnp.bfloat16)
 
 
 def whiten_bands(offsets, outs, table, raw_traces, channel_mask):
@@ -94,7 +95,7 @@
     return pl.pallas_call(
         functools.partial(spectra_kernel, offsets, outs),
         out_shape=[
-            jax.ShapeDtypeStruct(((stop - start) * ROWS, CH), jnp.bfloat16) for _, start, stop in outs
+            jax.ShapeDtypeStruct((len(runs) * BAND * ROWS, CH), jnp.bfloat16) for runs in outs
         ],
         in_specs=[anywhere] * 3,
         out_specs=[pl.BlockSpec(memory_space=pltpu.VMEM)] * len(outs),
@@ -118,43 +119,59 @@
     )(table, raw_traces, channel_mask)
 
 
-def cross_kernel(bins, *refs):
-    own_refs, other_refs, out_ref = refs[:BANDS], refs[BANDS : 2 * BANDS], refs[-1]
+def cross_kernel(first, last, starts, *refs):
+    count = len(starts)
+    piece_refs, out_ref, tiles, sems = refs[:count], refs[-3], refs[-2], refs[-1]
     scale = 1.0 / math.sqrt(WINS * BANDS)
-    for index in range(bins):
-        rows = slice(index * ROWS, (index + 1) * ROWS)
-        own = [ref[rows, :] for ref in own_refs]
-        turned = []
-        for piece in own:
-            turned += [piece[WINS:], -piece[:WINS]]
-        left = jnp.concatenate([jnp.concatenate(own, axis=0), jnp.concatenate(turned, axis=0)], axis=1)
-        right = jnp.concatenate([ref[rows, :] for ref in other_refs], axis=0)
-        tile = lax.dot_general(left, right, (((0,), (0,)), ((), ())), preferred_element_type=jnp.float32)
-        tile = (tile * scale).astype(jnp.bfloat16)
-        out_ref[index, 0] = tile[:CH]
-        out_ref[index, 1] = tile[CH:]
+
+    def copy_out(chunk):
+        bins = pl.ds(chunk * CHUNK, CHUNK)
+        to = pl.ds(first + chunk * CHUNK, CHUNK)
+        return pltpu.make_async_copy(tiles.at[bins], out_ref.at[to], sems.at[chunk])
+
+    @pl.loop(0, (last - first) // CHUNK)
+    def _(chunk):
+        for index in range(CHUNK):
+            bin_index = chunk * CHUNK + index
+            pieces = [
+                ref[pl.ds(pl.multiple_of((first - start + bin_index) * ROWS, ROWS), ROWS), :]
+                for ref, start in zip(piece_refs, starts)
+            ]
+            own, other = pieces[:BANDS], pieces[BANDS:]
+            turned = []
+            for piece in own:
+                turned += [piece[WINS:], -piece[:WINS]]
+            left = jnp.concatenate([jnp.concatenate(own, axis=0), jnp.concatenate(turned, axis=0)], axis=1)
+            right = jnp.concatenate(other, axis=0)
+            tile = lax.dot_general(left, right, (((0,), (0,)), ((), ())), preferred_element_type=jnp.float32)
+            tile = (tile * scale).astype(jnp.bfloat16)
+            tiles[bin_index, 0] = tile[:CH]
+            tiles[bin_index, 1] = tile[CH:]
+        copy_out(chunk).start()
+
+    @pl.loop(0, (last - first) // CHUNK)
+    def _(chunk):
+        copy_out(chunk).wait()
 
 
 def cross_blocks(own, other, first, last, into=None):
-    bins = STEP
-    steps = (last - first) // bins
-
-    def piece(start):
-        return pl.BlockSpec((bins * ROWS, CH), lambda step: ((first - start) // bins + step, 0))
-
-    arrays = list(own) + [array for array, _ in other]
-    in_specs = [piece(0)] * BANDS + [piece(start) for _, start in other]
+    arrays = [array for array, _ in own + other]
+    starts = tuple(start for _, start in own + other)
+    in_specs = [pl.BlockSpec(memory_space=pltpu.VMEM)] * len(arrays)
     aliases = {}
     if into is not None:
         aliases = {len(arrays): 0}
         arrays.append(into)
-        in_specs.append(pl.BlockSpec(memory_space=pl.ANY))
+        in_specs.append(pl.BlockSpec(memory_space=pltpu.HBM))
     return pl.pallas_call(
-        functools.partial(cross_kernel, bins),
+        functools.partial(cross_kernel, first, last, starts),
         out_shape=jax.ShapeDtypeStruct((BAND, 2, CH, CH), jnp.bfloat16),
-        grid=(steps,),
         in_specs=in_specs,
-        out_specs=pl.BlockSpec((bins, 2, CH, CH), lambda step: (first // bins + step, 0, 0, 0)),
+        out_specs=pl.BlockSpec(memory_space=pltpu.HBM),
+        scratch_shapes=[
+            pltpu.VMEM((last - first, 2, CH, CH), jnp.bfloat16),
+            pltpu.SemaphoreType.DMA(((last - first) // CHUNK,)),
+        ],
         input_output_aliases=aliases,
         compiler_params=pltpu.CompilerParams(vmem_limit_bytes=VMEM_LIMIT),
         cost_estimate=pl.CostEstimate(
@@ -165,12 +182,16 @@
     )(*arrays)
 
 
-def swap_win(piece, offset):
-    return lax.ppermute(piece, "win", [(i, i ^ offset) for i in range(lax.axis_size("win"))])
+def swap(piece, stride, offset):
+    blks, wins = lax.axis_size("blk"), lax.axis_size("win")
+    route = [
+        (blk * wins + win, (blk ^ stride) * wins + (win ^ offset)) for blk in range(blks) for win in range(wins)
+    ]
+    return lax.ppermute(piece, ("blk", "win"), route)
 
 
 def swap_blk(piece, stride):
-    return lax.ppermute(piece, "blk", [(i, i ^ stride) for i in range(lax.axis_size("blk"))])
+    return swap(piece, stride, 0)
 
 
 def tie(*arrays):
@@ -180,25 +201,25 @@
 def body(raw_traces, channel_mask):
     table = jnp.asarray(band_twiddles())
     far = lax.axis_size("blk") // 2
-    split = HEAD * ROWS
-    pieces = tuple((part, 0, BAND) for part in range(BANDS))
-    own0, leaving1, leaving2, leaving3 = whiten_bands(tuple(range(BANDS)), pieces, table, raw_traces, channel_mask)
-    far0 = swap_blk(own0, far)
-    own3, own2, own1 = swap_win(leaving3, 3), swap_win(leaving2, 2), swap_win(leaving1, 1)
-    head = jnp.concatenate([own2[:split], own3[:split]])
-    tail = jnp.concatenate([own2[split:], own3[split:]])
-    near0 = swap_blk(own0, 1)
-    far1 = swap_blk(own1, far)
-    own1_next, far0, near0 = tie(own1, far0, near0)
-    near1 = swap_blk(own1_next, 1)
-    near23 = swap_blk(jnp.concatenate([own2, own3]), 1)
-    far_head, far_tail = swap_blk(head, far), swap_blk(tail, far)
-    own = (own0, own1, own2, own3)
-    far_pieces = [(far0, 0), (far1, 0)]
-    second = cross_blocks(own, [(near0, 0), (near1, 0), (near23, 0), (near23, -BAND)], 0, BAND)
-    far_head, second = tie(far_head, second)
-    first = cross_blocks(own, far_pieces + [(far_head, 0), (far_head, -HEAD)], 0, HEAD)
-    first = cross_blocks(own, far_pieces + [(far_tail, HEAD), (far_tail, 2 * HEAD - BAND)], HEAD, BAND, first)
+    rows = BAND * ROWS
+    own0, leaving2, leaving13 = whiten_bands((0, 1, 2, 3), ((0,), (2,), (1, 3)), table, raw_traces, channel_mask)
+    from_core = swap(leaving13, 0, 1)
+    own1 = from_core[:rows]
+    same = jnp.concatenate([own0, own1])
+    cross = jnp.concatenate([leaving2, from_core[rows:]])
+    far01 = swap(same, far, 0)
+    far23 = swap(cross, far, 2)
+    arrived = swap(cross, 0, 2)
+    own2, own3 = arrived[:rows], arrived[rows:]
+    own0_next, arrived = tie(own0, arrived)
+    near0, near1 = swap_blk(own0_next, 1), swap_blk(own1, 1)
+    near2, near3 = swap_blk(own2, 1), swap_blk(own3, 1)
+    near = [(near0, 0), (near1, 0), (near2, 0), (near3, 0)]
+    own = [(same, 0), (same, -BAND), (arrived, 0), (arrived, -BAND)]
+    second = cross_blocks(own, near, 0, BAND)
+    far01, far23, second = tie(far01, far23, second)
+    far_pieces = [(far01, 0), (far01, -BAND), (far23, 0), (far23, -BAND)]
+    first = cross_blocks(own, far_pieces, 0, BAND)
     return first, second
 
 

time: 117 us -> 115 us (0.983)
  the two profiles are of different devices: /device:TPU:1 before, /device:TPU:38 now
where the time goes in v3:
time: 115 us
  waiting for transfers between devices  86.4 us (75%)
  Pallas kernels  13.9 us (12%)
  starting transfers between devices  13.6 us (12%)
    ppermute x8, waiting for transfers between devices, swap(): return lax.ppermute(piece, ('blk', 'win'), route)  86.4 us
    ppermute x8, starting transfers between devices, swap(): return lax.ppermute(piece, ('blk', 'win'), route)  13.6 us
    pallas_call x2, Pallas kernels, cross_blocks(): pl.pallas_call(functools.partial(cross_kernel, first, last, starts), out_...  7.12 us
    pallas_call x1, Pallas kernels, whiten_bands(): pl.pallas_call(functools.partial(spectra_kernel, offsets, outs), out_shap...  6.74 us
  transfers between devices with their start and end apart: 8, of which 6 were waited for; matrix products, arithmetic and copies ran while one was open for 0% of the time, Pallas kernels for 3%

profile of v3, /device:TPU:38, one launch (start us, length us, event | category | flops | bytes accessed | tf_op | source)
XLA Modules:
  0.0 114.8 jit_solution(14677323487251078438)
XLA Ops:
  0.6 6.7 %shard_map.50 = (bf16[2048,128]{1,0:T(8,128)(2,1)}, bf16[2048,128]{1,0:T(8,128)(2,1)}, bf16[4096,128]{1,0:T(8,128)(2,1)}) custom-call(bf16[4,128,1024]{2,1,0:T(8,128)(2,1)} %constant.2.clone.table_ref, bf16[16,1024,128]{2,1,0:T(8,128)(2,1)} %raw_ref.1, s32[16,128]{1,0:T(8,128)} %mask_ref.1), custom_call_target="tpu_custom_call" | custom-call | flops 2147483648 | bytes 6291456 | tf_op jit(solution)/shard_map/pallas_call | solution.py:95
  7.4 0.0 copy-start.1
  7.4 0.0 copy-start
  7.4 0.1 collective-permute-start
  7.5 2.9 %collective-permute-done = bf16[4096,128]{1,0:T(8,128)(2,1)S(1)} collective-permute-done((bf16[4096,128]{1,0:T(8,128)(2,1)}, bf16[4096,128]{1,0:T(8,128)(2,1)S(1)}, u32[]{:S(2)}, u32[]{:S(2)}) %collective-permute-start) | collective-permute-done | bytes 1048608 | tf_op jit(solution)/shard_map/ppermute | solution.py:190
  10.4 0.1 fusion.1
  10.4 0.0 copy-done.1
  10.4 0.1 pad_maximum_fusion.1
  10.5 3.3 %collective-permute-start.1 = (bf16[4096,128]{1,0:T(8,128)(2,1)S(1)}, bf16[4096,128]{1,0:T(8,128)(2,1)S(1)}, u32[]{:S(2)}, u32[]{:S(2)}) collective-permute-start(bf16[4096,128]{1,0:T(8,128)(2,1)S(1)} %pad_maximum_fusion.1), channel_id=1, source_target_pairs={{0,2},{1,3},{2,0},{3,1},{4,6},{5,7},{6,4},{7,5},{8,10},{9,11},{10,... | collective-permute-start | bytes 3145736 | tf_op jit(solution)/shard_map/ppermute | solution.py:190
  13.8 6.1 %collective-permute-start.3 = (bf16[4096,128]{1,0:T(8,128)(2,1)S(1)}, bf16[4096,128]{1,0:T(8,128)(2,1)S(1)}, u32[]{:S(2)}, u32[]{:S(2)}) collective-permute-start(bf16[4096,128]{1,0:T(8,128)(2,1)S(1)} %pad_maximum_fusion.1), channel_id=1, source_target_pairs={{0,130},{1,131},{2,128},{3,129},{4,134},{5,135},{6,132},{7,133},{8... | collective-permute-start | bytes 3145736 | tf_op jit(solution)/shard_map/ppermute | solution.py:190
  19.9 0.8 collective-permute-start.5
  20.7 0.0 copy-done
  20.7 0.1 pad_maximum_fusion.refs_0_.refs_1_
  20.8 0.3 collective-permute-start.2
  21.1 28.0 %collective-permute-done.1.refs_2_.refs_3_ = bf16[4096,128]{1,0:T(8,128)(2,1)S(1)} collective-permute-done((bf16[4096,128]{1,0:T(8,128)(2,1)S(1)}, bf16[4096,128]{1,0:T(8,128)(2,1)S(1)}, u32[]{:S(2)}, u32[]{:S(2)}) %collective-permute-start.1) | collective-permute-done | bytes 1048608 | tf_op jit(solution)/shard_map/ppermute | solution.py:190
  49.1 0.9 collective-permute-start.4
  50.0 0.1 fusion
  50.1 1.2 %collective-permute-start.7 = (bf16[2048,128]{1,0:T(8,128)(2,1)S(1)}, bf16[2048,128]{1,0:T(8,128)(2,1)S(1)}, u32[]{:S(2)}, u32[]{:S(2)}) collective-permute-start(bf16[2048,128]{1,0:T(8,128)(2,1)S(1)} %get-tuple-element.18), channel_id=1, source_target_pairs={{0,4},{1,5},{2,6},{3,7},{4,0},{5,1},{6,2},{7,3},{8,12},{9,13},{10,... | collective-permute-start | bytes 1572872 | tf_op jit(solution)/shard_map/ppermute | solution.py:190
  51.3 0.0 collective-permute-done.5.refs_5_
  51.3 0.9 collective-permute-start.6
  52.2 11.8 %collective-permute-done.4.refs_4_ = bf16[2048,128]{1,0:T(8,128)(2,1)S(1)} collective-permute-done((bf16[2048,128]{1,0:T(8,128)(2,1)S(1)}, bf16[2048,128]{1,0:T(8,128)(2,1)S(1)}, u32[]{:S(2)}, u32[]{:S(2)}) %collective-permute-start.4) | collective-permute-done | bytes 524320 | tf_op jit(solution)/shard_map/ppermute | solution.py:190
  64.0 11.2 %collective-permute-done.7.refs_7_ = bf16[2048,128]{1,0:T(8,128)(2,1)S(1)} collective-permute-done((bf16[2048,128]{1,0:T(8,128)(2,1)S(1)}, bf16[2048,128]{1,0:T(8,128)(2,1)S(1)}, u32[]{:S(2)}, u32[]{:S(2)}) %collective-permute-start.7) | collective-permute-done | bytes 524320 | tf_op jit(solution)/shard_map/ppermute | solution.py:190
  75.2 9.4 %collective-permute-done.6.refs_6_ = bf16[2048,128]{1,0:T(8,128)(2,1)S(1)} collective-permute-done((bf16[2048,128]{1,0:T(8,128)(2,1)S(1)}, bf16[2048,128]{1,0:T(8,128)(2,1)S(1)}, u32[]{:S(2)}, u32[]{:S(2)}) %collective-permute-start.6) | collective-permute-done | bytes 524320 | tf_op jit(solution)/shard_map/ppermute | solution.py:190
  84.6 3.6 %shard_map.51 = bf16[64,2,128,128]{3,2,1,0:T(8,128)(2,1)} custom-call(bf16[4096,128]{1,0:T(8,128)(2,1)S(1)} %pad_maximum_fusion.refs_0_.refs_1_, bf16[4096,128]{1,0:T(8,128)(2,1)S(1)} %pad_maximum_fusion.refs_0_.refs_1_, bf16[4096,128]{1,0:T(8,128)(2,1)S(1)} %collective-permute-done.1.refs_2_.refs_3_, ...), custom_call_target="tpu_custom_call" | custom-call | flops 536870912 | bytes 8388608 | tf_op jit(solution)/shard_map/pallas_call | solution.py:166
  88.1 23.1 %collective-permute-done.2.refs_4_.refs_5_ = bf16[4096,128]{1,0:T(8,128)(2,1)S(1)} collective-permute-done((bf16[4096,128]{1,0:T(8,128)(2,1)S(1)}, bf16[4096,128]{1,0:T(8,128)(2,1)S(1)}, u32[]{:S(2)}, u32[]{:S(2)}) %collective-permute-start.2) | collective-permute-done | bytes 1048608 | tf_op jit(solution)/shard_map/ppermute | solution.py:190
  111.3 0.0 collective-permute-done.3.refs_6_.refs_7_
  111.3 3.6 %shard_map.52 = bf16[64,2,128,128]{3,2,1,0:T(8,128)(2,1)} custom-call(bf16[4096,128]{1,0:T(8,128)(2,1)S(1)} %pad_maximum_fusion.refs_0_.refs_1_, bf16[4096,128]{1,0:T(8,128)(2,1)S(1)} %pad_maximum_fusion.refs_0_.refs_1_, bf16[4096,128]{1,0:T(8,128)(2,1)S(1)} %collective-permute-done.1.refs_2_.refs_3_, ...), custom_call_target="tpu_custom_call" | custom-call | flops 536870912 | bytes 8388608 | tf_op jit(solution)/shard_map/pallas_call | solution.py:166
Async XLA Ops:
  7.4 3.1 %copy-start.1 = (bf16[2048,128]{1,0:T(8,128)(2,1)S(1)}, bf16[2048,128]{1,0:T(8,128)(2,1)}, u32[]{:S(2)}) copy-start(bf16[2048,128]{1,0:T(8,128)(2,1)} %get-tuple-element.12) | copy-start | bytes 1572868
  7.4 13.3 %copy-start = (bf16[2048,128]{1,0:T(8,128)(2,1)S(1)}, bf16[2048,128]{1,0:T(8,128)(2,1)}, u32[]{:S(2)}) copy-start(bf16[2048,128]{1,0:T(8,128)(2,1)} %get-tuple-element.14) | copy-start | bytes 1572868
  7.4 3.0 %collective-permute-start = (bf16[4096,128]{1,0:T(8,128)(2,1)}, bf16[4096,128]{1,0:T(8,128)(2,1)S(1)}, u32[]{:S(2)}, u32[]{:S(2)}) collective-permute-start(bf16[4096,128]{1,0:T(8,128)(2,1)} %get-tuple-element.11), channel_id=1, source_target_pairs={{0,1},{1,0},{2,3},{3,2},{4,5},{5,4},{6,7},{7,6},{8,9},{9,8},{10,11... | collective-permute-start | bytes 3145736 | tf_op jit(solution)/shard_map/ppermute | solution.py:190
  10.5 38.6 %collective-permute-start.1 = (bf16[4096,128]{1,0:T(8,128)(2,1)S(1)}, bf16[4096,128]{1,0:T(8,128)(2,1)S(1)}, u32[]{:S(2)}, u32[]{:S(2)}) collective-permute-start(bf16[4096,128]{1,0:T(8,128)(2,1)S(1)} %pad_maximum_fusion.1), channel_id=1, source_target_pairs={{0,2},{1,3},{2,0},{3,1},{4,6},{5,7},{6,4},{7,5},{8,10},{9,11},{10,... | collective-permute-start | bytes 3145736 | tf_op jit(solution)/shard_map/ppermute | solution.py:190
  13.8 97.5 %collective-permute-start.3 = (bf16[4096,128]{1,0:T(8,128)(2,1)S(1)}, bf16[4096,128]{1,0:T(8,128)(2,1)S(1)}, u32[]{:S(2)}, u32[]{:S(2)}) collective-permute-start(bf16[4096,128]{1,0:T(8,128)(2,1)S(1)} %pad_maximum_fusion.1), channel_id=1, source_target_pairs={{0,130},{1,131},{2,128},{3,129},{4,134},{5,135},{6,132},{7,133},{8... | collective-permute-start | bytes 3145736 | tf_op jit(solution)/shard_map/ppermute | solution.py:190
  19.9 31.4 %collective-permute-start.5 = (bf16[2048,128]{1,0:T(8,128)(2,1)S(1)}, bf16[2048,128]{1,0:T(8,128)(2,1)S(1)}, u32[]{:S(2)}, u32[]{:S(2)}) collective-permute-start(bf16[2048,128]{1,0:T(8,128)(2,1)S(1)} %get-tuple-element.21), channel_id=1, source_target_pairs={{0,4},{1,5},{2,6},{3,7},{4,0},{5,1},{6,2},{7,3},{8,12},{9,13},{10,... | collective-permute-start | bytes 1572872 | tf_op jit(solution)/shard_map/ppermute | solution.py:190
  20.8 90.5 %collective-permute-start.2 = (bf16[4096,128]{1,0:T(8,128)(2,1)S(1)}, bf16[4096,128]{1,0:T(8,128)(2,1)S(1)}, u32[]{:S(2)}, u32[]{:S(2)}) collective-permute-start(bf16[4096,128]{1,0:T(8,128)(2,1)S(1)} %pad_maximum_fusion.refs_0_.refs_1_), channel_id=1, source_target_pairs={{0,128},{1,129},{2,130},{3,131},{4,132},{5,133},{6,134},{7,135},{8... | collective-permute-start | bytes 3145736 | tf_op jit(solution)/shard_map/ppermute | solution.py:190
  49.1 14.9 %collective-permute-start.4 = (bf16[2048,128]{1,0:T(8,128)(2,1)S(1)}, bf16[2048,128]{1,0:T(8,128)(2,1)S(1)}, u32[]{:S(2)}, u32[]{:S(2)}) collective-permute-start(bf16[2048,128]{1,0:T(8,128)(2,1)S(1)} %copy-done), channel_id=1, source_target_pairs={{0,4},{1,5},{2,6},{3,7},{4,0},{5,1},{6,2},{7,3},{8,12},{9,13},{10,... | collective-permute-start | bytes 1572872 | tf_op jit(solution)/shard_map/ppermute | solution.py:190
  50.1 25.1 %collective-permute-start.7 = (bf16[2048,128]{1,0:T(8,128)(2,1)S(1)}, bf16[2048,128]{1,0:T(8,128)(2,1)S(1)}, u32[]{:S(2)}, u32[]{:S(2)}) collective-permute-start(bf16[2048,128]{1,0:T(8,128)(2,1)S(1)} %get-tuple-element.18), channel_id=1, source_target_pairs={{0,4},{1,5},{2,6},{3,7},{4,0},{5,1},{6,2},{7,3},{8,12},{9,13},{10,... | collective-permute-start | bytes 1572872 | tf_op jit(solution)/shard_map/ppermute | solution.py:190
  51.3 33.3 %collective-permute-start.6 = (bf16[2048,128]{1,0:T(8,128)(2,1)S(1)}, bf16[2048,128]{1,0:T(8,128)(2,1)S(1)}, u32[]{:S(2)}, u32[]{:S(2)}) collective-permute-start(bf16[2048,128]{1,0:T(8,128)(2,1)S(1)} %get-tuple-element.19), channel_id=1, source_target_pairs={{0,4},{1,5},{2,6},{3,7},{4,0},{5,1},{6,2},{7,3},{8,12},{9,13},{10,... | collective-permute-start | bytes 1572872 | tf_op jit(solution)/shard_map/ppermute | solution.py:190

commit v4 on v3

--- a/solution.py
+++ b/solution.py
@@ -121,7 +121,9 @@
 
 def cross_kernel(first, last, starts, *refs):
     count = len(starts)
-    piece_refs, out_ref, tiles, sems = refs[:count], refs[-3], refs[-2], refs[-1]
+    piece_refs, out_ref, left_ref, tiles, sems = refs[:count], refs[-4], refs[-3], refs[-2], refs[-1]
+    if count == BANDS:
+        left_ref, out_ref = refs[count], refs[-3]
     scale = 1.0 / math.sqrt(WINS * BANDS)
 
     def copy_out(chunk):
@@ -137,13 +139,15 @@
                 ref[pl.ds(pl.multiple_of((first - start + bin_index) * ROWS, ROWS), ROWS), :]
                 for ref, start in zip(piece_refs, starts)
             ]
-            own, other = pieces[:BANDS], pieces[BANDS:]
-            turned = []
-            for piece in own:
-                turned += [piece[WINS:], -piece[:WINS]]
-            left = jnp.concatenate([jnp.concatenate(own, axis=0), jnp.concatenate(turned, axis=0)], axis=1)
-            right = jnp.concatenate(other, axis=0)
-            tile = lax.dot_general(left, right, (((0,), (0,)), ((), ())), preferred_element_type=jnp.float32)
+            right = jnp.concatenate(pieces[-BANDS:], axis=0)
+            if count > BANDS:
+                own = pieces[:BANDS]
+                turned = []
+                for piece in own:
+                    turned += [piece[WINS:], -piece[:WINS]]
+                left = jnp.concatenate([jnp.concatenate(own, axis=0), jnp.concatenate(turned, axis=0)], axis=1)
+                left_ref[bin_index] = left.T
+            tile = jnp.dot(left_ref[bin_index], right, preferred_element_type=jnp.float32)
             tile = (tile * scale).astype(jnp.bfloat16)
             tiles[bin_index, 0] = tile[:CH]
             tiles[bin_index, 1] = tile[CH:]
@@ -154,25 +158,25 @@
         copy_out(chunk).wait()
 
 
-def cross_blocks(own, other, first, last, into=None):
-    arrays = [array for array, _ in own + other]
-    starts = tuple(start for _, start in own + other)
+def cross_blocks(own, other, first, last, left=None):
+    pieces = own + other if left is None else other
+    arrays = [array for array, _ in pieces] + ([] if left is None else [left])
+    starts = tuple(start for _, start in pieces)
     in_specs = [pl.BlockSpec(memory_space=pltpu.VMEM)] * len(arrays)
-    aliases = {}
-    if into is not None:
-        aliases = {len(arrays): 0}
-        arrays.append(into)
-        in_specs.append(pl.BlockSpec(memory_space=pltpu.HBM))
+    out_shape = [jax.ShapeDtypeStruct((BAND, 2, CH, CH), jnp.bfloat16)]
+    out_specs = [pl.BlockSpec(memory_space=pltpu.HBM)]
+    if left is None:
+        out_shape.append(jax.ShapeDtypeStruct((BAND, 2 * CH, ROWS * BANDS), jnp.bfloat16))
+        out_specs.append(pl.BlockSpec(memory_space=pltpu.VMEM))
     return pl.pallas_call(
         functools.partial(cross_kernel, first, last, starts),
-        out_shape=jax.ShapeDtypeStruct((BAND, 2, CH, CH), jnp.bfloat16),
+        out_shape=out_shape,
         in_specs=in_specs,
-        out_specs=pl.BlockSpec(memory_space=pltpu.HBM),
+        out_specs=out_specs,
         scratch_shapes=[
             pltpu.VMEM((last - first, 2, CH, CH), jnp.bfloat16),
             pltpu.SemaphoreType.DMA(((last - first) // CHUNK,)),
         ],
-        input_output_aliases=aliases,
         compiler_params=pltpu.CompilerParams(vmem_limit_bytes=VMEM_LIMIT),
         cost_estimate=pl.CostEstimate(
             flops=2 * (last - first) * 2 * CH * CH * 2 * WINS * BANDS,
@@ -216,10 +220,10 @@
     near2, near3 = swap_blk(own2, 1), swap_blk(own3, 1)
     near = [(near0, 0), (near1, 0), (near2, 0), (near3, 0)]
     own = [(same, 0), (same, -BAND), (arrived, 0), (arrived, -BAND)]
-    second = cross_blocks(own, near, 0, BAND)
+    second, left = cross_blocks(own, near, 0, BAND)
     far01, far23, second = tie(far01, far23, second)
     far_pieces = [(far01, 0), (far01, -BAND), (far23, 0), (far23, -BAND)]
-    first = cross_blocks(own, far_pieces, 0, BAND)
+    (first,) = cross_blocks(own, far_pieces, 0, BAND, left)
     return first, second
 
 

time: 115 us -> 115 us (level)
  no operation moved by 1% of the time
where the time goes in v4:
time: 115 us; the launch traced here: 114 us
  waiting for transfers between devices  86 us (75%)
  Pallas kernels  13.9 us (12%)
  starting transfers between devices  13.6 us (12%)
    ppermute x8, waiting for transfers between devices, swap(): return lax.ppermute(piece, ('blk', 'win'), route)  86 us
    ppermute x8, starting transfers between devices, swap(): return lax.ppermute(piece, ('blk', 'win'), route)  13.6 us
    pallas_call x2, Pallas kernels, cross_blocks(): pl.pallas_call(functools.partial(cross_kernel, first, last, starts), out_...  7.11 us
    pallas_call x1, Pallas kernels, whiten_bands(): pl.pallas_call(functools.partial(spectra_kernel, offsets, outs), out_shap...  6.74 us
  transfers between devices with their start and end apart: 8, of which 6 were waited for; matrix products, arithmetic and copies ran while one was open for 0% of the time, Pallas kernels for 3%

profile of v4, /device:TPU:38, one launch (start us, length us, event | category | flops | bytes accessed | tf_op | source)
XLA Modules:
  0.0 114.5 jit_solution(15568787238830746859)
XLA Ops:
  0.6 6.7 %shard_map.50 = (bf16[2048,128]{1,0:T(8,128)(2,1)}, bf16[2048,128]{1,0:T(8,128)(2,1)}, bf16[4096,128]{1,0:T(8,128)(2,1)}) custom-call(bf16[4,128,1024]{2,1,0:T(8,128)(2,1)} %constant.2.clone.table_ref, bf16[16,1024,128]{2,1,0:T(8,128)(2,1)} %raw_ref.1, s32[16,128]{1,0:T(8,128)} %mask_ref.1), custom_call_target="tpu_custom_call" | custom-call | flops 2147483648 | bytes 6291456 | tf_op jit(solution)/shard_map/pallas_call | solution.py:95
  7.4 0.0 copy-start.1
  7.4 0.0 copy-start
  7.4 0.1 collective-permute-start
  7.5 2.9 %collective-permute-done = bf16[4096,128]{1,0:T(8,128)(2,1)S(1)} collective-permute-done((bf16[4096,128]{1,0:T(8,128)(2,1)}, bf16[4096,128]{1,0:T(8,128)(2,1)S(1)}, u32[]{:S(2)}, u32[]{:S(2)}) %collective-permute-start) | collective-permute-done | bytes 1048608 | tf_op jit(solution)/shard_map/ppermute | solution.py:194
  10.4 0.1 fusion.1
  10.4 0.0 copy-done.1
  10.4 0.1 pad_maximum_fusion.1
  10.5 3.3 %collective-permute-start.3 = (bf16[4096,128]{1,0:T(8,128)(2,1)S(1)}, bf16[4096,128]{1,0:T(8,128)(2,1)S(1)}, u32[]{:S(2)}, u32[]{:S(2)}) collective-permute-start(bf16[4096,128]{1,0:T(8,128)(2,1)S(1)} %pad_maximum_fusion.1), channel_id=1, source_target_pairs={{0,2},{1,3},{2,0},{3,1},{4,6},{5,7},{6,4},{7,5},{8,10},{9,11},{10,... | collective-permute-start | bytes 3145736 | tf_op jit(solution)/shard_map/ppermute | solution.py:194
  13.8 6.1 %collective-permute-start.2 = (bf16[4096,128]{1,0:T(8,128)(2,1)S(1)}, bf16[4096,128]{1,0:T(8,128)(2,1)S(1)}, u32[]{:S(2)}, u32[]{:S(2)}) collective-permute-start(bf16[4096,128]{1,0:T(8,128)(2,1)S(1)} %pad_maximum_fusion.1), channel_id=1, source_target_pairs={{0,130},{1,131},{2,128},{3,129},{4,134},{5,135},{6,132},{7,133},{8... | collective-permute-start | bytes 3145736 | tf_op jit(solution)/shard_map/ppermute | solution.py:194
  19.9 0.8 collective-permute-start.5
  20.7 0.0 copy-done
  20.7 0.1 pad_maximum_fusion.refs_0_.refs_1_
  20.8 0.3 collective-permute-start.1
  21.1 28.0 %collective-permute-done.3.refs_2_.refs_3_ = bf16[4096,128]{1,0:T(8,128)(2,1)S(1)} collective-permute-done((bf16[4096,128]{1,0:T(8,128)(2,1)S(1)}, bf16[4096,128]{1,0:T(8,128)(2,1)S(1)}, u32[]{:S(2)}, u32[]{:S(2)}) %collective-permute-start.3) | collective-permute-done | bytes 1048608 | tf_op jit(solution)/shard_map/ppermute | solution.py:194
  49.1 0.9 collective-permute-start.4
  50.0 0.1 fusion
  50.1 1.2 %collective-permute-start.7 = (bf16[2048,128]{1,0:T(8,128)(2,1)S(1)}, bf16[2048,128]{1,0:T(8,128)(2,1)S(1)}, u32[]{:S(2)}, u32[]{:S(2)}) collective-permute-start(bf16[2048,128]{1,0:T(8,128)(2,1)S(1)} %get-tuple-element.22), channel_id=1, source_target_pairs={{0,4},{1,5},{2,6},{3,7},{4,0},{5,1},{6,2},{7,3},{8,12},{9,13},{10,... | collective-permute-start | bytes 1572872 | tf_op jit(solution)/shard_map/ppermute | solution.py:194
  51.3 0.0 collective-permute-done.5.refs_5_
  51.3 0.9 collective-permute-start.6
  52.2 11.8 %collective-permute-done.4.refs_4_ = bf16[2048,128]{1,0:T(8,128)(2,1)S(1)} collective-permute-done((bf16[2048,128]{1,0:T(8,128)(2,1)S(1)}, bf16[2048,128]{1,0:T(8,128)(2,1)S(1)}, u32[]{:S(2)}, u32[]{:S(2)}) %collective-permute-start.4) | collective-permute-done | bytes 524320 | tf_op jit(solution)/shard_map/ppermute | solution.py:194
  64.0 11.2 %collective-permute-done.7.refs_7_ = bf16[2048,128]{1,0:T(8,128)(2,1)S(1)} collective-permute-done((bf16[2048,128]{1,0:T(8,128)(2,1)S(1)}, bf16[2048,128]{1,0:T(8,128)(2,1)S(1)}, u32[]{:S(2)}, u32[]{:S(2)}) %collective-permute-start.7) | collective-permute-done | bytes 524320 | tf_op jit(solution)/shard_map/ppermute | solution.py:194
  75.2 9.4 %collective-permute-done.6.refs_6_ = bf16[2048,128]{1,0:T(8,128)(2,1)S(1)} collective-permute-done((bf16[2048,128]{1,0:T(8,128)(2,1)S(1)}, bf16[2048,128]{1,0:T(8,128)(2,1)S(1)}, u32[]{:S(2)}, u32[]{:S(2)}) %collective-permute-start.6) | collective-permute-done | bytes 524320 | tf_op jit(solution)/shard_map/ppermute | solution.py:194
  84.6 3.9 %shard_map.51 = (bf16[64,2,128,128]{3,2,1,0:T(8,128)(2,1)}, bf16[64,256,128]{2,1,0:T(8,128)(2,1)S(1)}) custom-call(bf16[4096,128]{1,0:T(8,128)(2,1)S(1)} %pad_maximum_fusion.refs_0_.refs_1_, bf16[4096,128]{1,0:T(8,128)(2,1)S(1)} %pad_maximum_fusion.refs_0_.refs_1_, bf16[4096,128]{1,0:T(8,128)(2,1)S(1)} %collective-permute-done.3.refs_2_.refs_3_, ...), custom_call_target="tpu_custom_call" | custom-call | flops 536870912 | bytes 8388608 | tf_op jit(solution)/shard_map/pallas_call | solution.py:171
  88.5 22.8 %collective-permute-done.1.refs_0_.refs_1_ = bf16[4096,128]{1,0:T(8,128)(2,1)S(1)} collective-permute-done((bf16[4096,128]{1,0:T(8,128)(2,1)S(1)}, bf16[4096,128]{1,0:T(8,128)(2,1)S(1)}, u32[]{:S(2)}, u32[]{:S(2)}) %collective-permute-start.1) | collective-permute-done | bytes 1048608 | tf_op jit(solution)/shard_map/ppermute | solution.py:194
  111.3 0.0 collective-permute-done.2.refs_2_.refs_3_
  111.3 3.2 %shard_map.52 = bf16[64,2,128,128]{3,2,1,0:T(8,128)(2,1)} custom-call(bf16[4096,128]{1,0:T(8,128)(2,1)S(1)} %collective-permute-done.1.refs_0_.refs_1_, bf16[4096,128]{1,0:T(8,128)(2,1)S(1)} %collective-permute-done.1.refs_0_.refs_1_, bf16[4096,128]{1,0:T(8,128)(2,1)S(1)} %collective-permute-done.2.refs_2_.refs_3_, ...), custom_call_target="tpu_custom_call" | custom-call | flops 536870912 | bytes 8388608 | tf_op jit(solution)/shard_map/pallas_call | solution.py:171
Async XLA Ops:
  7.4 3.1 %copy-start.1 = (bf16[2048,128]{1,0:T(8,128)(2,1)S(1)}, bf16[2048,128]{1,0:T(8,128)(2,1)}, u32[]{:S(2)}) copy-start(bf16[2048,128]{1,0:T(8,128)(2,1)} %get-tuple-element.14) | copy-start | bytes 1572868
  7.4 13.3 %copy-start = (bf16[2048,128]{1,0:T(8,128)(2,1)S(1)}, bf16[2048,128]{1,0:T(8,128)(2,1)}, u32[]{:S(2)}) copy-start(bf16[2048,128]{1,0:T(8,128)(2,1)} %get-tuple-element.16) | copy-start | bytes 1572868
  7.4 3.0 %collective-permute-start = (bf16[4096,128]{1,0:T(8,128)(2,1)}, bf16[4096,128]{1,0:T(8,128)(2,1)S(1)}, u32[]{:S(2)}, u32[]{:S(2)}) collective-permute-start(bf16[4096,128]{1,0:T(8,128)(2,1)} %get-tuple-element.13), channel_id=1, source_target_pairs={{0,1},{1,0},{2,3},{3,2},{4,5},{5,4},{6,7},{7,6},{8,9},{9,8},{10,11... | collective-permute-start | bytes 3145736 | tf_op jit(solution)/shard_map/ppermute | solution.py:194
  10.5 38.6 %collective-permute-start.3 = (bf16[4096,128]{1,0:T(8,128)(2,1)S(1)}, bf16[4096,128]{1,0:T(8,128)(2,1)S(1)}, u32[]{:S(2)}, u32[]{:S(2)}) collective-permute-start(bf16[4096,128]{1,0:T(8,128)(2,1)S(1)} %pad_maximum_fusion.1), channel_id=1, source_target_pairs={{0,2},{1,3},{2,0},{3,1},{4,6},{5,7},{6,4},{7,5},{8,10},{9,11},{10,... | collective-permute-start | bytes 3145736 | tf_op jit(solution)/shard_map/ppermute | solution.py:194
  13.8 97.5 %collective-permute-start.2 = (bf16[4096,128]{1,0:T(8,128)(2,1)S(1)}, bf16[4096,128]{1,0:T(8,128)(2,1)S(1)}, u32[]{:S(2)}, u32[]{:S(2)}) collective-permute-start(bf16[4096,128]{1,0:T(8,128)(2,1)S(1)} %pad_maximum_fusion.1), channel_id=1, source_target_pairs={{0,130},{1,131},{2,128},{3,129},{4,134},{5,135},{6,132},{7,133},{8... | collective-permute-start | bytes 3145736 | tf_op jit(solution)/shard_map/ppermute | solution.py:194
  19.9 31.4 %collective-permute-start.5 = (bf16[2048,128]{1,0:T(8,128)(2,1)S(1)}, bf16[2048,128]{1,0:T(8,128)(2,1)S(1)}, u32[]{:S(2)}, u32[]{:S(2)}) collective-permute-start(bf16[2048,128]{1,0:T(8,128)(2,1)S(1)} %get-tuple-element.25), channel_id=1, source_target_pairs={{0,4},{1,5},{2,6},{3,7},{4,0},{5,1},{6,2},{7,3},{8,12},{9,13},{10,... | collective-permute-start | bytes 1572872 | tf_op jit(solution)/shard_map/ppermute | solution.py:194
  20.8 90.5 %collective-permute-start.1 = (bf16[4096,128]{1,0:T(8,128)(2,1)S(1)}, bf16[4096,128]{1,0:T(8,128)(2,1)S(1)}, u32[]{:S(2)}, u32[]{:S(2)}) collective-permute-start(bf16[4096,128]{1,0:T(8,128)(2,1)S(1)} %pad_maximum_fusion.refs_0_.refs_1_), channel_id=1, source_target_pairs={{0,128},{1,129},{2,130},{3,131},{4,132},{5,133},{6,134},{7,135},{8... | collective-permute-start | bytes 3145736 | tf_op jit(solution)/shard_map/ppermute | solution.py:194
  49.1 14.9 %collective-permute-start.4 = (bf16[2048,128]{1,0:T(8,128)(2,1)S(1)}, bf16[2048,128]{1,0:T(8,128)(2,1)S(1)}, u32[]{:S(2)}, u32[]{:S(2)}) collective-permute-start(bf16[2048,128]{1,0:T(8,128)(2,1)S(1)} %copy-done), channel_id=1, source_target_pairs={{0,4},{1,5},{2,6},{3,7},{4,0},{5,1},{6,2},{7,3},{8,12},{9,13},{10,... | collective-permute-start | bytes 1572872 | tf_op jit(solution)/shard_map/ppermute | solution.py:194
  50.1 25.1 %collective-permute-start.7 = (bf16[2048,128]{1,0:T(8,128)(2,1)S(1)}, bf16[2048,128]{1,0:T(8,128)(2,1)S(1)}, u32[]{:S(2)}, u32[]{:S(2)}) collective-permute-start(bf16[2048,128]{1,0:T(8,128)(2,1)S(1)} %get-tuple-element.22), channel_id=1, source_target_pairs={{0,4},{1,5},{2,6},{3,7},{4,0},{5,1},{6,2},{7,3},{8,12},{9,13},{10,... | collective-permute-start | bytes 1572872 | tf_op jit(solution)/shard_map/ppermute | solution.py:194
  51.3 33.3 %collective-permute-start.6 = (bf16[2048,128]{1,0:T(8,128)(2,1)S(1)}, bf16[2048,128]{1,0:T(8,128)(2,1)S(1)}, u32[]{:S(2)}, u32[]{:S(2)}) collective-permute-start(bf16[2048,128]{1,0:T(8,128)(2,1)S(1)} %get-tuple-element.23), channel_id=1, source_target_pairs={{0,4},{1,5},{2,6},{3,7},{4,0},{5,1},{6,2},{7,3},{8,12},{9,13},{10,... | collective-permute-start | bytes 1572872 | tf_op jit(solution)/shard_map/ppermute | solution.py:194
